TPU v7x, 32 devices: a whole 2x2x4 slice. The times are simulated.
32 devices in a mesh: blk: 4 (over x, core), uly: 2 (over y), tp: 4 (over z).
Axes of the slice: x: 2, y: 2, z: 4, core: 2. Of those that a mesh axis runs over, the one named last changes fastest.
Arguments:
- hidden: bfloat16 [4096, 8192], P(('blk', 'uly')), may hold values from -8 to 8
- norm_gain: bfloat16 [8192], replicated, may hold values from 0.099609375 to 1.8984375
- query_key_value_weight: bfloat16 [8192, 4, 1280], P('uly', 'tp'), may hold values from -1 to 1
- w_out: bfloat16 [4096, 8192], P('tp', 'uly'), may hold values from -0.5 to 0.5
- doc_ids: int32 [4096], replicated, may hold values from 0 to 7, never falling along the last dimension, each value on 1 to 2048 neighbouring positions
- block_order: int32 [8], replicated, may hold values from 0 to 7, each once
Outputs:
- attn_out: bfloat16 [4096, 8192], P(('blk', 'tp'), 'uly')
Inputs may be any that keep to these rules, and one draw needn't show every extreme that they name: `doc_ids`: never falls along the sequence; every document holds 1 to 2048 positions and one holds exactly 2048. Array rows c * 512 to (c + 1) * 512 - 1 hold sequence block block_order[c]; every block appears once.
All inputs are finite; a program needn't handle non-finite values.
Results may differ from a plain program's by a relative error of at most 0.029.
Values may be sent and summed in bfloat16 or wider, within the bound.
No kernel may reach another device: no remote copies, remote signals or barrier semaphores. Data moves between devices by JAX's collectives and lax.ppermute only.
A program may use at most 128 MiB of HBM per device.

v0:
```python
import functools
import math

import jax
import jax.numpy as jnp
from jax import lax
from jax.experimental import pallas as pl
from jax.experimental.pallas import tpu as pltpu
from jax.sharding import PartitionSpec as P

QUERY_HEAD_COUNT = 32
KV_HEAD_COUNT = 4
HEAD_SIZE = 128
BLOCK = 512
GROUP_WIDTH = QUERY_HEAD_COUNT // KV_HEAD_COUNT

COST = dict(
    norm=4e+09,
    pair=1e+09,
    queries_a=4e+09,
    att_a0=4e+09,
    queries_b=1e+06,
    att_b0=4e+09,
    att_b1=4e+09,
    out=4e+09,
)
THETA = 500000.0
NEG_BIG = -1e30


def rope_tables(positions):
    half_dim = HEAD_SIZE // 2
    lane_ids = jnp.arange(half_dim).astype(jnp.float32)
    base_freq = jnp.power(THETA, -2.0 * lane_ids / HEAD_SIZE)
    wavelen = 2.0 * math.pi / base_freq
    smooth = (8192.0 / wavelen - 1.0) / 3.0
    blended = (1.0 - smooth) * base_freq / 8.0 + smooth * base_freq
    scaled = jnp.where(
        wavelen > 8192.0, base_freq / 8.0, jnp.where(wavelen < 2048.0, base_freq, blended)
    )
    angles = positions.astype(jnp.float32)[:, None] * scaled[None, :]
    return (jnp.cos(angles), jnp.sin(angles))


VMEM = pl.BlockSpec(memory_space=pltpu.VMEM)
SMEM = pl.BlockSpec(memory_space=pltpu.SMEM)
HBM = pl.BlockSpec(memory_space=pltpu.HBM)


def call(kernel, specs, shapes, operands, cost, scratch=(), vmem=16):
    return pl.pallas_call(
        kernel,
        in_specs=specs,
        out_specs=[VMEM] * len(shapes),
        out_shape=[jax.ShapeDtypeStruct(shape, dtype) for shape, dtype in shapes],
        scratch_shapes=scratch,
        compiler_params=pltpu.CompilerParams(vmem_limit_bytes=vmem * 1024 * 1024),
        cost_estimate=pl.CostEstimate(flops=int(cost), bytes_accessed=0, transcendentals=0),
    )(*operands)


def norm_kernel(start_ref, hidden_ref, gain_ref, own_ref, rest_ref, tiles, sems):
    slots, tile = tiles.shape[:2]
    steps = own_ref.shape[0] // tile
    run = rest_ref.shape[1] // 4

    def fetch(i):
        return pltpu.make_async_copy(
            hidden_ref.at[pl.ds(i * tile, tile), :], tiles.at[i % slots], sems.at[i % slots]
        )

    for i in range(slots):
        fetch(i).start()
    for i in range(steps):
        fetch(i).wait()
        widened = tiles[i % slots].astype(jnp.float32)
        inverse_rms = lax.rsqrt(jnp.mean(widened * widened, axis=1, keepdims=True) + 1e-05)
        rows = pl.ds(i * tile, tile)

        def write(ref, lane, start, size):
            lanes = pl.ds(pl.multiple_of(start, 512), size)
            part = tiles[i % slots, :, lanes].astype(jnp.float32)
            gain = gain_ref[:, lanes].astype(jnp.float32)
            ref[rows, lane : lane + size] = (part * inverse_rms * gain).astype(jnp.bfloat16)

        write(own_ref, 0, start_ref[0], own_ref.shape[1])
        for j in range(4):
            write(rest_ref, j * run, start_ref[1 + j], run)
        if i + slots < steps:
            fetch(i + slots).start()


def norm_rows(starts, hidden, gain):
    rows, width = hidden.shape
    tile, slots = 64, 4
    return call(
        norm_kernel,
        [SMEM, HBM, VMEM],
        [((rows, w), jnp.bfloat16) for w in (width // 2, width // 2)],
        (starts, hidden, gain.reshape(1, width)),
        COST["norm"],
        [pltpu.VMEM((slots, tile, width), jnp.bfloat16), pltpu.SemaphoreType.DMA((slots,))],
        vmem=50,
    )


def proj_kernel(first_column, rotated, own_ref, rest_ref, *refs):
    pieces, refs = refs[:4], refs[4:]
    weights_ref, cos_ref, sin_ref, out_ref, scratch, sems = refs
    depth, columns = scratch.shape
    part = depth // 4
    copies = [
        pltpu.make_async_copy(
            weights_ref.at[pl.ds(i * part, part), pl.ds(first_column, columns)],
            scratch.at[pl.ds(i * part, part)],
            sems.at[i],
        )
        for i in range(4)
    ]
    for copy in copies:
        copy.start()
    total = None
    for i, piece in enumerate(pieces):
        run = piece.shape[0]
        product = jnp.dot(
            rest_ref[:, i * run : (i + 1) * run], piece[...], preferred_element_type=jnp.float32
        )
        total = product if total is None else total + product
    for copy in copies:
        copy.wait()
    total += jnp.dot(own_ref[...], scratch[...], preferred_element_type=jnp.float32)
    for i in range(columns // HEAD_SIZE):
        lanes = slice(i * HEAD_SIZE, (i + 1) * HEAD_SIZE)
        head = total[:, lanes]
        if i < rotated:
            head = head * cos_ref[...] + pltpu.roll(head, HEAD_SIZE // 2, 1) * sin_ref[...]
        out_ref[:, lanes] = head.astype(jnp.bfloat16)


def project(cost, own, rest, pieces, weights, first_column, rotated, tables):
    rows = own.shape[0]
    columns = pieces[0].shape[1]
    return call(
        functools.partial(proj_kernel, first_column, rotated),
        [*[VMEM] * 6, HBM, VMEM, VMEM],
        [((rows, columns), jnp.bfloat16)],
        (own, rest, *pieces, weights, *tables),
        COST[cost],
        [pltpu.VMEM((weights.shape[0], columns), jnp.bfloat16), pltpu.SemaphoreType.DMA((4,))],
        vmem=40,
    )[0]


def attend_kernel(count, first_head, runs, info_ref, q_ref, first_ref, *refs):
    near = refs[:count]
    out_ref, m_ref, l_ref, acc_ref = refs[count:]
    my_block = info_ref[0]
    first_block = info_ref[1]
    scale = math.log2(math.e) / math.sqrt(HEAD_SIZE)
    rows, columns = out_ref.shape
    heads = columns // HEAD_SIZE

    def take(ref, lanes):
        pieces = [ref[start : start + size, lanes] for start, size in runs]
        return pieces[0] if len(pieces) == 1 else jnp.concatenate(pieces, axis=0)

    queries = [
        take(q_ref, slice((first_head + h) * HEAD_SIZE, (first_head + h + 1) * HEAD_SIZE))
        for h in range(heads)
    ]
    firsts = [first_ref[:, start : start + size] for start, size in runs]
    firsts = firsts[0] if len(firsts) == 1 else jnp.concatenate(firsts, axis=1)

    def one_block(block, diagonal):
        slot = info_ref[2 + block]
        begin = pl.multiple_of((slot % (8 // count)) * BLOCK, BLOCK)
        pair = near[0][pl.ds(begin, BLOCK), :]
        for i in range(1, count):
            pair = jnp.where(slot // (8 // count) == i, near[i][pl.ds(begin, BLOCK), :], pair)
        keys, values = pair[:, :HEAD_SIZE], pair[:, HEAD_SIZE:].T
        place = lax.broadcasted_iota(jnp.int32, (BLOCK, rows), 0)
        allowed = place >= firsts - block * BLOCK
        if diagonal:
            ranges = [
                lax.broadcasted_iota(jnp.int32, (BLOCK, size), 1) + start for start, size in runs
            ]
            ranges = ranges[0] if len(ranges) == 1 else jnp.concatenate(ranges, axis=1)
            allowed &= place <= ranges
        for h in range(heads):
            scores = lax.dot_general(
                keys, queries[h], (((1,), (1,)), ((), ())), preferred_element_type=jnp.float32
            )
            scores = jnp.where(allowed, scores, NEG_BIG)
            new_max = jnp.max(scores, axis=0, keepdims=True)
            if not diagonal:
                old_max = m_ref[h]
                new_max = jnp.maximum(old_max, new_max)
            weights = jnp.exp2((scores - new_max) * scale)
            block_sum = jnp.sum(weights, axis=0, keepdims=True)
            product = jnp.dot(
                values, weights.astype(jnp.bfloat16), preferred_element_type=jnp.float32
            )
            if diagonal:
                l_ref[h] = block_sum
                acc_ref[h] = product
            else:
                factor = jnp.exp2((old_max - new_max) * scale)
                l_ref[h] = l_ref[h] * factor + block_sum
                acc_ref[h] = acc_ref[h] * factor + product
            m_ref[h] = new_max

    one_block(my_block, True)

    def body(i, carry):
        one_block(my_block - i, False)
        return carry

    lax.fori_loop(1, my_block - first_block + 1, body, 0)
    for h in range(heads):
        lanes = slice(h * HEAD_SIZE, (h + 1) * HEAD_SIZE)
        out_ref[:, lanes] = (acc_ref[h] / l_ref[h]).T.astype(jnp.bfloat16)


def attend(cost, info, queries, pairs, first_key, first_head, heads, runs):
    rows = sum(size for _, size in runs)
    return call(
        functools.partial(attend_kernel, len(pairs), first_head, runs),
        [SMEM, VMEM, VMEM, *[VMEM] * len(pairs)],
        [((rows, heads * HEAD_SIZE), jnp.bfloat16)],
        (info, queries, first_key, *pairs),
        COST[cost],
        [
            pltpu.VMEM((heads, 1, rows), jnp.float32),
            pltpu.VMEM((heads, 1, rows), jnp.float32),
            pltpu.VMEM((heads, HEAD_SIZE, rows), jnp.float32),
        ],
    )[0]


def out_kernel(first_column, all_runs, info_ref, *refs):
    parts = len(all_runs)
    mine, theirs, far = (refs[i * parts : (i + 1) * parts] for i in range(3))
    quarters = refs[3 * parts : 3 * parts + 4]
    own_ref, keep_ref, send_ref, own_weights, lhs, total, sem = refs[3 * parts + 4 :]
    half, columns = keep_ref.shape
    copy = pltpu.make_async_copy(own_ref.at[:, pl.ds(first_column, columns)], own_weights, sem)
    copy.start()

    def gather(pieces):
        lane = 0
        for piece, runs in zip(pieces, all_runs):
            width, row = piece.shape[1], 0
            for start, size in runs:
                lhs[row : row + size, lane : lane + width] = piece[start : start + size, :]
                row += size
            lane += width

    gather(far)
    products = []
    for i, quarter in enumerate(quarters):
        depth = quarter.shape[0]
        heads = pl.ds(pl.multiple_of(info_ref[2 + i], depth), depth)
        products.append(
            jnp.dot(lhs[:, heads], quarter[...], preferred_element_type=jnp.float32)
        )
    total[...] = sum(products[1:], products[0])

    @pl.when(info_ref[0] == 1)
    def _():
        gather(mine)

    @pl.when(info_ref[0] == 0)
    def _():
        gather(theirs)

    copy.wait()
    total[...] += jnp.dot(lhs[...], own_weights[...], preferred_element_type=jnp.float32)
    keep_at = pl.multiple_of(info_ref[1] * half, half)
    keep_ref[...] = total[pl.ds(keep_at, half), :]
    send_ref[...] = total[pl.ds(half - keep_at, half), :].astype(jnp.bfloat16)


def project_out(info, mine, theirs, far, all_runs, quarters, own, first_column):
    rows = sum(size for _, size in all_runs[0])
    depth, columns = own.shape[0], quarters[0].shape[1]
    half = rows // 2
    return call(
        functools.partial(out_kernel, first_column, all_runs),
        [SMEM, *[VMEM] * (3 * len(mine) + 4), HBM],
        [((half, columns), jnp.float32), ((half, columns), jnp.bfloat16)],
        (info, *mine, *theirs, *far, *quarters, own),
        COST["out"],
        [
            pltpu.VMEM((depth, columns), jnp.bfloat16),
            pltpu.VMEM((rows, depth), jnp.bfloat16),
            pltpu.VMEM((rows, columns), jnp.float32),
            pltpu.SemaphoreType.DMA,
        ],
        vmem=36,
    )


def after(array, *others):
    return lax.optimization_barrier((array, *others))[0]


def swap_uly(array):
    return lax.ppermute(array, "uly", [(0, 1), (1, 0)])


def swap(array, name, bit):
    return lax.ppermute(array, name, [(i, i ^ bit) for i in range(4)])


def pick(table, index):
    ids = jnp.arange(table.shape[0])
    return jnp.sum(jnp.where(index[..., None] == ids, table, 0), axis=-1)


def one_block_each(hidden, norm_gain, query_key_value_weight, w_out, doc_ids, block_order):
    blk, uly, tp = (lax.axis_index(name) for name in ("blk", "uly", "tp"))
    weights = query_key_value_weight.reshape(query_key_value_weight.shape[0], -1)
    depth = weights.shape[0] // 4
    nblocks = block_order.shape[0]
    peers = blk ^ jnp.array([0, 2, 1, 3])
    query_width = GROUP_WIDTH * HEAD_SIZE
    part = query_width // 2
    out_depth, out_width = w_out.shape
    out_part = out_width // 2

    def take(start, size, first_column, columns):
        return lax.dynamic_slice(weights, (blk * depth + start, first_column), (size, columns))

    def take_out(p):
        return lax.dynamic_slice(
            w_out, (blk * (out_depth // 4), p * out_part), (out_depth // 4, out_part)
        )

    def across(piece):
        return swap(piece, "blk", 1)

    def along(piece):
        return swap(piece, "blk", 2)

    pair_y = swap_uly(take(0, depth, query_width, 2 * HEAD_SIZE))
    a, b = (take(0, depth, p * part, part) for p in range(2))

    def two_along_tp(piece):
        return lax.all_gather(piece, "tp", axis=0, axis_index_groups=[[0, 2], [1, 3]])

    def other(both):
        return lax.dynamic_index_in_dim(both, 1 - tp // 2, 0, keepdims=False)

    w0, w1 = take_out(0), take_out(1)
    a_y = swap_uly(a)
    w0_both, w1_both = two_along_tp(w0), two_along_tp(w1)

    my_row = blk * 2 + uly
    my_block = pick(block_order, my_row)
    positions = my_block * BLOCK + jnp.arange(BLOCK)
    cosine, sine = rope_tables(positions)
    tables = (
        jnp.concatenate([cosine, cosine], axis=1),
        jnp.concatenate([-sine, sine], axis=1),
    )

    pair_y = after(pair_y, a, b, w0, w1, *tables)
    pair_yx = along(pair_y)
    base = (uly * weights.shape[0])[None]
    starts = jnp.concatenate([base, (1 - uly) * weights.shape[0] + peers * depth])
    own, rest = norm_rows(starts, after(hidden, pair_y), norm_gain)

    pieces = [pair_y, pair_yx, across(pair_y), across(after(pair_yx, rest))]
    pair = project("pair", own, rest, pieces, weights, query_width, 1, tables)
    pair_x = along(pair)
    pair_c = across(pair)
    block_order, doc_ids = after(block_order, pair), after(doc_ids, pair)
    rows_of_slots = jnp.stack(
        [(blk ^ c ^ x) * 2 + (uly ^ u) for c in (0, 1) for u in (0, 1) for x in (0, 2)]
    )
    blocks_of_slots = pick(block_order, rows_of_slots)
    slots = jnp.arange(nblocks)
    slot_of_block = jnp.sum(
        jnp.where(blocks_of_slots[None, :] == slots[:, None], slots[None, :], 0), axis=1
    )
    query_seg = lax.dynamic_slice(doc_ids, (my_block * BLOCK,), (BLOCK,))
    first_key = jnp.sum((doc_ids[:, None] < query_seg[None, :]).astype(jnp.int32), axis=0)
    info = jnp.concatenate([jnp.stack([my_block, first_key[0] // BLOCK]), slot_of_block])
    first_key = first_key[None, :]


    w0_z = other(after(w0_both, pair))
    a_y = after(a_y, pair_c)
    a_yx = along(a_y)
    b_y = swap_uly(b)
    two = jnp.concatenate([pair, pair_x], axis=0)
    two_y = swap_uly(after(two, info))
    pieces = [a_y, a_yx, across(a_y), across(a_yx)]
    b_y = after(b_y, pair_x)
    b_yx = along(b_y)
    queries_a = project(
        "queries_a", own, after(rest, b_y, w0_z), pieces, weights, 0, 4, tables
    )
    two_y = after(two_y, queries_a)
    pairs = (
        jnp.concatenate([two, two_y], axis=0),
        jnp.concatenate([pair_c, across(pair_x), across(two_y)], axis=0),
    )
    att_a = attend("att_a0", info, queries_a, pairs, first_key, 0, 4, ((0, BLOCK),))
    att_a_y = swap_uly(att_a)
    use_own = (uly == 0) == (tp < 2)

    pieces = [b_y, b_yx, across(b_y), across(after(b_yx, att_a))]
    queries_b = project(
        "queries_b", own, after(rest, att_a), pieces, weights, part, 4, tables
    )
    w1_z = other(after(w1_both, queries_b))
    w0_z = after(w0_z, att_a)
    w0_zx = along(w0_z)
    far_a = swap(jnp.where(use_own, att_a_y, att_a), "tp", 2)

    quarter = BLOCK // 4
    halves = [((h * quarter, quarter), ((2 + h) * quarter, quarter)) for h in range(2)]
    att_b, att_b_y, far_b = [], [], []
    ready = after(info, att_a_y, *([w1_z] if 1==2 else []))
    for h in range(2):
        att_b.append(attend(f"att_b{h}", ready, queries_b, pairs, first_key, 0, 4, halves[h]))
        att_b_y.append(swap_uly(att_b[h]))
        ready = after(info, att_b[0], far_a, w1_z)
    for h in range(2):
        sent = jnp.where(use_own, att_b_y[h], att_b[h])
        far_b.append(swap(sent, "tp", 2))
    w1_z = after(w1_z, att_b[0])
    w1_zx = along(w1_z)

    late = queries_b
    w_quarters = [
        [w0_z, w0_zx, across(after(w0_z, late)), across(after(w0_zx, late))],
        [w1_z, w1_zx, across(after(w1_z, late)), across(after(w1_zx, late))],
    ]
    out_info = jnp.concatenate(
        [jnp.stack([use_own.astype(jnp.int32), tp % 2]), peers * (out_depth // 4)]
    )
    results = []
    for h in range(2):
        runs = (halves[h], ((0, BLOCK // 2),))
        line = []
        for p in range(2):
            keep, send = project_out(
                out_info,
                (att_a, att_b[h]),
                (att_a_y, att_b_y[h]),
                (far_a, far_b[h]),
                runs,
                w_quarters[p],
                w_out,
                p * out_part,
            )
            got = swap(send, "tp", 1)
            line.append((keep + got.astype(jnp.float32)).astype(jnp.bfloat16))
        results.append(jnp.concatenate(line, axis=1))
    return jnp.concatenate(results, axis=0)


def rotate(values, cos_table, sin_table):
    half_dim = values.shape[-1] // 2
    leading = values[..., :half_dim]
    trailing = values[..., half_dim:]
    cos_part = cos_table[:, None, :]
    sin_part = sin_table[:, None, :]
    return jnp.concatenate(
        [leading * cos_part - trailing * sin_part, trailing * cos_part + leading * sin_part],
        axis=-1,
    )


def positions_of(block_order, row_ids):
    block_ids = row_ids // BLOCK
    matches = block_ids[:, None] == jnp.arange(block_order.shape[0])[None, :]
    seq_block = jnp.sum(jnp.where(matches, block_order[None, :], 0), axis=1)
    return seq_block * BLOCK + row_ids % BLOCK


def make_attend(queries, query_pos, query_seg, doc_ids, block_order):
    head_dim = queries.shape[2]
    inv_root = 1.0 / math.sqrt(head_dim)

    def attend_pieces(running, pieces):
        key_piece, value_piece = pieces
        key_count = key_piece.shape[0]
        block_size = key_count
        while block_size > 1024 and block_size % 2 == 0:
            block_size = block_size // 2
        block_total = key_count // block_size
        piece_pos = positions_of(block_order, jnp.arange(key_count))
        piece_seg = jnp.take(doc_ids, piece_pos)
        stacked = (
            key_piece.reshape(block_total, block_size, head_dim),
            value_piece.reshape(block_total, block_size, head_dim),
            piece_pos.reshape(block_total, block_size),
            piece_seg.reshape(block_total, block_size),
        )

        def one_block(softmax_state, block_data):
            key_blk, value_blk, pos_blk, seg_blk = block_data
            allowed = (pos_blk[None, :] <= query_pos[:, None]) & (
                seg_blk[None, :] == query_seg[:, None]
            )
            row_max, row_sum, weighted = softmax_state
            scores = (
                jnp.einsum("qhd,kd->hqk", queries, key_blk, preferred_element_type=jnp.float32)
                * inv_root
            )
            scores = jnp.where(allowed[None, :, :], scores, NEG_BIG)
            new_max = jnp.maximum(row_max, jnp.max(scores, axis=2))
            weights = jnp.where(allowed[None, :, :], jnp.exp(scores - new_max[:, :, None]), 0.0)
            factor = jnp.exp(row_max - new_max)
            new_sum = row_sum * factor + jnp.sum(weights, axis=2)
            product = jnp.einsum(
                "hqk,kd->hqd",
                weights.astype(jnp.bfloat16),
                value_blk,
                preferred_element_type=jnp.float32,
            )
            next_state = (new_max, new_sum, weighted * factor[:, :, None] + product)
            return (next_state, None)

        final_state, unused = lax.scan(one_block, running, stacked)
        return final_state

    return attend_pieces


def on_device(hidden, norm_gain, query_key_value_weight, w_out, doc_ids, block_order):
    group_width = GROUP_WIDTH
    heads_here = group_width // lax.axis_size("uly")
    widened = hidden.astype(jnp.float32)
    inverse_rms = lax.rsqrt(jnp.mean(widened * widened, axis=1, keepdims=True) + 1e-05)
    rms_scaled = (widened * inverse_rms * norm_gain.astype(jnp.float32)[None, :]).astype(
        jnp.bfloat16
    )
    regrouped = lax.all_to_all(rms_scaled, "uly", split_axis=1, concat_axis=0, tiled=True)
    block_len = regrouped.shape[0]
    local_weights = query_key_value_weight.reshape(
        query_key_value_weight.shape[0], (group_width + 2) * HEAD_SIZE
    )
    partial_proj = jnp.dot(regrouped, local_weights, preferred_element_type=jnp.float32)
    query_part = partial_proj[:, : group_width * HEAD_SIZE]
    pair_part = partial_proj[:, group_width * HEAD_SIZE :]
    first_row = lax.axis_index("blk") * block_len
    query_pos = positions_of(block_order, first_row + jnp.arange(block_len))
    query_seg = jnp.take(doc_ids, query_pos)
    cos_query, sin_query = rope_tables(query_pos)
    query_sum, pair_sum = (
        lax.psum_scatter(query_part, "uly", scatter_dimension=1, tiled=True),
        lax.psum_scatter(pair_part, "uly", scatter_dimension=0, tiled=True),
    )
    key_len = pair_sum.shape[0]
    key_start = first_row + lax.axis_index("uly") * key_len
    key_pos = positions_of(block_order, key_start + jnp.arange(key_len))
    cos_key, sin_key = rope_tables(key_pos)
    queries = rotate(
        query_sum.reshape(block_len, heads_here, HEAD_SIZE), cos_query, sin_query
    ).astype(jnp.bfloat16)
    keys_local = rotate(pair_sum[:, None, :HEAD_SIZE], cos_key, sin_key)[:, 0, :].astype(
        jnp.bfloat16
    )
    values_local = pair_sum[:, HEAD_SIZE:].astype(jnp.bfloat16)
    attend_pieces = make_attend(queries, query_pos, query_seg, doc_ids, block_order)
    initial = (
        jnp.full((heads_here, block_len), NEG_BIG, jnp.float32),
        jnp.zeros((heads_here, block_len), jnp.float32),
        jnp.zeros((heads_here, block_len, HEAD_SIZE), jnp.float32),
    )
    row_max, row_sum, weighted = attend_pieces(
        initial,
        (
            lax.all_gather(keys_local, ("blk", "uly"), axis=0, tiled=True),
            lax.all_gather(values_local, ("blk", "uly"), axis=0, tiled=True),
        ),
    )
    attended = (weighted / row_sum[:, :, None]).astype(jnp.bfloat16)
    head_weights = w_out.reshape(group_width, HEAD_SIZE, w_out.shape[1])
    projected_rows = jnp.einsum(
        "hqd,hdn->qn",
        lax.all_gather(attended, "uly", axis=0, tiled=True),
        head_weights,
        preferred_element_type=jnp.float32,
    )
    return lax.psum_scatter(
        projected_rows.astype(jnp.bfloat16), "tp", scatter_dimension=0, tiled=True
    )


def solution(mesh):
    sizes = dict(mesh.shape)

    def whole(hidden, *rest):
        tokens = hidden.shape[0]
        fits = (sizes["blk"], sizes["uly"], sizes["tp"]) == (4, 2, 4) and tokens == 8 * BLOCK
        return jax.shard_map(
            one_block_each if fits else on_device,
            mesh=mesh,
            in_specs=(P(("blk", "uly"), None), P(), P("uly", "tp", None), P("tp", "uly"), P(), P()),
            out_specs=P(("blk", "tp"), "uly"),
            check_vma=False,
        )(hidden, *rest)

    return whole
```

profile of v0, /device:TPU:0, one launch (start us, length us, event | category | flops | bytes accessed | tf_op | source)
XLA Modules:
  0.0 259.0 jit_solution(12260668545771456826)
XLA Ops:
  7.6 3.0 %collective-permute-start = (bf16[1024,256]{1,0:T(8,128)(2,1)S(1)}, bf16[1024,256]{1,0:T(8,128)(2,1)S(1)}, u32[]{:S(2)}, u32[]{:S(2)}) collective-permute-start(bf16[1024,256]{1,0:T(8,128)(2,1)S(1)} %dynamic-slice_bitcast_fusion.4), channel_id=1, source_target_pairs={{0,4},{4,0},{1,5},{5,1},{2,6},{6,2},{3,7},{7,3},{8,12},{12,8},{9,1... | collective-permute-start | bytes 1572872 | tf_op jit(solution)/shard_map/ppermute | solution.py:308
  10.7 3.1 %constant_dynamic-slice_fusion.1 = (bf16[256,2048]{1,0:T(8,128)(2,1)}, bf16[256,2048]{1,0:T(8,128)(2,1)}) fusion(bf16[1024,4096]{1,0:T(8,128)(2,1)} %refs_10_.7, s32[]{:T(128)S(6)} %select_n.82), kind=kLoop, calls=%fused_computation.40 | loop fusion | bytes 4194308 | tf_op jit(solution)/shard_map/dynamic_slice | solution.py:335
  13.8 3.0 %dynamic-slice_bitcast_fusion.2 = (bf16[1024,512]{1,0:T(8,128)(2,1)}, bf16[1024,512]{1,0:T(8,128)(2,1)}) fusion(bf16[4096,1,1280]{2,0,1:T(8,128)(2,1)} %param.9, s32[]{:T(128)S(6)} %select_n.81), kind=kLoop, calls=%fused_computation.9 | loop fusion | bytes 4194308 | tf_op jit(solution)/shard_map/dynamic_slice | solution.py:332
  19.5 3.9 %collective-permute-done.refs_0_ = bf16[1024,256]{1,0:T(8,128)(2,1)S(1)} collective-permute-done((bf16[1024,256]{1,0:T(8,128)(2,1)S(1)}, bf16[1024,256]{1,0:T(8,128)(2,1)S(1)}, u32[]{:S(2)}, u32[]{:S(2)}) %collective-permute-start) | collective-permute-done | bytes 524320 | tf_op jit(solution)/shard_map/ppermute | solution.py:308
  25.6 10.0 %shard_map.73 = (bf16[512,4096]{1,0:T(8,128)(2,1)}, bf16[512,4096]{1,0:T(8,128)(2,1)}) custom-call(s32[5]{0:T(128)S(1)} %pad_add_fusion.1.start_ref, bf16[512,8192]{1,0:T(8,128)(2,1)} %hidden_ref, bf16[1,8192]{1,0:T(2,128)(2,1)S(1)} %reshape.41.gain_ref), custom_call_target="tpu_custom_call" | custom-call | flops 4000000000 | tf_op jit(solution)/shard_map/pallas_call | solution.py:51
  37.7 2.2 copy-done.1
  39.9 2.2 copy-done.4
  42.1 6.0 %shard_map.74 = bf16[512,256]{1,0:T(8,128)(2,1)S(1)} custom-call(bf16[512,4096]{1,0:T(8,128)(2,1)S(1)} %copy-done.1, bf16[512,4096]{1,0:T(8,128)(2,1)S(1)} %copy-done.4, bf16[1024,256]{1,0:T(8,128)(2,1)S(1)} %collective-permute-done.refs_0_, bf16[1024,256]{1,0:T(8,128)(2,1)S(1)} %collective-permute-done.1.refs_1_, ...), custom_call_target="tpu_custom_call" | custom-call | flops 1000000000 | tf_op jit(solution)/shard_map/pallas_call | solution.py:51
  52.5 22.9 %collective-permute-done.8.refs_1_ = bf16[1024,512]{1,0:T(8,128)(2,1)} collective-permute-done((bf16[1024,512]{1,0:T(8,128)(2,1)}, bf16[1024,512]{1,0:T(8,128)(2,1)}, u32[]{:S(2)}, u32[]{:S(2)}) %collective-permute-start.8) | collective-permute-done | bytes 1048608 | tf_op jit(solution)/shard_map/ppermute | solution.py:312
  81.9 2.4 collective-permute-done.5
  92.7 7.0 %shard_map.75.q_ref = bf16[512,512]{1,0:T(8,128)(2,1)S(1)} custom-call(bf16[512,4096]{1,0:T(8,128)(2,1)S(1)} %copy-done.2, bf16[512,4096]{1,0:T(8,128)(2,1)S(1)} %copy-done.5, bf16[1024,512]{1,0:T(8,128)(2,1)} %collective-permute-done.6.refs_0_, bf16[1024,512]{1,0:T(8,128)(2,1)} %collective-permute-done.8.refs_1_, ...), custom_call_target="tpu_custom_call" | custom-call | flops 4000000000 | tf_op jit(solution)/shard_map/pallas_call | solution.py:51
  102.5 5.1 %shard_map.76.refs_0_ = bf16[512,512]{1,0:T(8,128)(2,1)S(1)} custom-call(s32[10]{0:T(128)S(1)} %pad_add_fusion.2.info_ref, bf16[512,512]{1,0:T(8,128)(2,1)S(1)} %shard_map.75.q_ref, s32[1,512]{1,0:T(1,128)S(1)} %bitcast.28, bf16[2048,256]{1,0:T(8,128)(2,1)S(1)} %pad_maximum_fusion.refs_0_, bf16[2048,256]{1,0:T(8,128)(2,1)S(1)} %constant_dynamic-update-slice_fusion.refs_1_), custom_call_target="tpu_custom_call" | custom-call | flops 4000000000 | tf_op jit(solution)/shard_map/pallas_call | solution.py:51
  107.6 3.2 %collective-permute-done.15.refs_1_ = bf16[1024,512]{1,0:T(8,128)(2,1)} collective-permute-done((bf16[1024,512]{1,0:T(8,128)(2,1)}, bf16[1024,512]{1,0:T(8,128)(2,1)}, u32[]{:S(2)}, u32[]{:S(2)}) %collective-permute-start.15) | collective-permute-done | bytes 1048608 | tf_op jit(solution)/shard_map/ppermute | solution.py:312
  110.8 5.3 %collective-permute-start.14 = (bf16[512,512]{1,0:T(8,128)(2,1)S(1)}, bf16[512,512]{1,0:T(8,128)(2,1)S(1)}, u32[]{:S(2)}, u32[]{:S(2)}) collective-permute-start(bf16[512,512]{1,0:T(8,128)(2,1)S(1)} %shard_map.76.refs_0_), channel_id=1, source_target_pairs={{0,4},{4,0},{1,5},{5,1},{2,6},{6,2},{3,7},{7,3},{8,12},{12,8},{9,1... | collective-permute-start | bytes 1572872 | tf_op jit(solution)/shard_map/ppermute | solution.py:308
  116.1 12.2 %collective-permute-done.14.refs_2_ = bf16[512,512]{1,0:T(8,128)(2,1)S(1)} collective-permute-done((bf16[512,512]{1,0:T(8,128)(2,1)S(1)}, bf16[512,512]{1,0:T(8,128)(2,1)S(1)}, u32[]{:S(2)}, u32[]{:S(2)}) %collective-permute-start.14) | collective-permute-done | bytes 524320 | tf_op jit(solution)/shard_map/ppermute | solution.py:308
  129.2 2.5 collective-permute-start.19
  136.1 7.0 %shard_map.77.q_ref = bf16[512,512]{1,0:T(8,128)(2,1)S(1)} custom-call(bf16[512,4096]{1,0:T(8,128)(2,1)S(1)} %copy-done.3, bf16[512,4096]{1,0:T(8,128)(2,1)S(1)} %copy-done.6, bf16[1024,512]{1,0:T(8,128)(2,1)} %collective-permute-done.4.refs_0_, bf16[1024,512]{1,0:T(8,128)(2,1)} %collective-permute-done.15.refs_1_, ...), custom_call_target="tpu_custom_call" | custom-call | flops 1000000 | tf_op jit(solution)/shard_map/pallas_call | solution.py:51
  148.7 4.3 %shard_map.78.refs_1_ = bf16[256,512]{1,0:T(8,128)(2,1)S(1)} custom-call(s32[10]{0:T(128)S(1)} %pad_add_fusion.2.info_ref, bf16[512,512]{1,0:T(8,128)(2,1)S(1)} %copy-done.10, s32[1,512]{1,0:T(1,128)S(1)} %bitcast.29, bf16[2048,256]{1,0:T(8,128)(2,1)S(1)} %copy-done.8, bf16[2048,256]{1,0:T(8,128)(2,1)S(1)} %copy-done.12), custom_call_target="tpu_custom_call" | custom-call | flops 4000000000 | tf_op jit(solution)/shard_map/pallas_call | solution.py:51
  152.9 2.5 collective-permute-done.19.refs_4_
  155.5 4.5 %collective-permute-start.25 = (bf16[256,2048]{1,0:T(8,128)(2,1)S(1)}, bf16[256,2048]{1,0:T(8,128)(2,1)}, u32[]{:S(2)}, u32[]{:S(2)}) collective-permute-start(bf16[256,2048]{1,0:T(8,128)(2,1)S(1)} %dynamic-slice_bitcast_fusion.refs_6_), channel_id=1, source_target_pairs={{0,16},{8,24},{16,0},{24,8},{1,17},{9,25},{17,1},{25,9},{2,18},{10... | collective-permute-start | bytes 3145736 | tf_op jit(solution)/shard_map/ppermute | solution.py:312
  160.5 4.9 %shard_map.81.refs_1_ = bf16[256,512]{1,0:T(8,128)(2,1)} custom-call(s32[10]{0:T(128)S(1)} %pad_add_fusion.2.info_ref, bf16[512,512]{1,0:T(8,128)(2,1)S(1)} %copy-done.10, s32[1,512]{1,0:T(1,128)S(1)} %bitcast.30, bf16[2048,256]{1,0:T(8,128)(2,1)S(1)} %copy-done.8, bf16[2048,256]{1,0:T(8,128)(2,1)S(1)} %copy-done.12), custom_call_target="tpu_custom_call" | custom-call | flops 4000000000 | tf_op jit(solution)/shard_map/pallas_call | solution.py:51
  167.4 4.7 %collective-permute-done.29.refs_3_ = bf16[256,512]{1,0:T(8,128)(2,1)} collective-permute-done((bf16[256,512]{1,0:T(8,128)(2,1)}, bf16[256,512]{1,0:T(8,128)(2,1)}, u32[]{:S(2)}, u32[]{:S(2)}) %collective-permute-start.29) | collective-permute-done | bytes 262176 | tf_op jit(solution)/shard_map/ppermute | solution.py:308
  175.1 5.4 %collective-permute-start.26 = (bf16[256,2048]{1,0:T(8,128)(2,1)S(1)}, bf16[256,2048]{1,0:T(8,128)(2,1)S(1)}, u32[]{:S(2)}, u32[]{:S(2)}) collective-permute-start(bf16[256,2048]{1,0:T(8,128)(2,1)S(1)} %dynamic-slice_bitcast_fusion.refs_6_), channel_id=1, source_target_pairs={{0,8},{8,0},{16,24},{24,16},{1,9},{9,1},{17,25},{25,17},{2,10},{10... | collective-permute-start | bytes 3145736 | tf_op jit(solution)/shard_map/ppermute | solution.py:312
  183.5 10.3 %collective-permute-start.27 = (bf16[256,2048]{1,0:T(8,128)(2,1)}, bf16[256,2048]{1,0:T(8,128)(2,1)S(1)}, u32[]{:S(2)}, u32[]{:S(2)}) collective-permute-start(bf16[256,2048]{1,0:T(8,128)(2,1)} %collective-permute-done.25.refs_7_), channel_id=1, source_target_pairs={{0,8},{8,0},{16,24},{24,16},{1,9},{9,1},{17,25},{25,17},{2,10},{10... | collective-permute-start | bytes 3145736 | tf_op jit(solution)/shard_map/ppermute | solution.py:312
  193.8 3.4 %copy-done = bf16[1024,4096]{1,0:T(8,128)(2,1)S(1)} copy-done((bf16[1024,4096]{1,0:T(8,128)(2,1)S(1)}, bf16[1024,4096]{1,0:T(8,128)(2,1)}, u32[]{:S(2)}) %copy-start) | copy-done | bytes 8388632
  197.2 5.8 %shard_map.82 = (f32[128,2048]{1,0:T(8,128)S(1)}, bf16[128,2048]{1,0:T(8,128)(2,1)S(1)}) custom-call(s32[6]{0:T(128)S(1)} %pad_add_fusion.info_ref, bf16[512,512]{1,0:T(8,128)(2,1)S(1)} %shard_map.76.refs_0_, bf16[256,512]{1,0:T(8,128)(2,1)} %shard_map.81.refs_1_, bf16[512,512]{1,0:T(8,128)(2,1)S(1)} %collective-permute-done.14.refs_2_, ...), custom_call_target="tpu_custom_call" | custom-call | flops 4000000000 | tf_op jit(solution)/shard_map/pallas_call | solution.py:51
  203.0 5.6 %shard_map.79 = (f32[128,2048]{1,0:T(8,128)S(1)}, bf16[128,2048]{1,0:T(8,128)(2,1)S(1)}) custom-call(s32[6]{0:T(128)S(1)} %pad_add_fusion.info_ref, bf16[512,512]{1,0:T(8,128)(2,1)S(1)} %shard_map.76.refs_0_, bf16[256,512]{1,0:T(8,128)(2,1)S(1)} %shard_map.78.refs_1_, bf16[512,512]{1,0:T(8,128)(2,1)S(1)} %collective-permute-done.14.refs_2_, ...), custom_call_target="tpu_custom_call" | custom-call | flops 4000000000 | tf_op jit(solution)/shard_map/pallas_call | solution.py:51
  210.7 7.1 %collective-permute-done.31 = bf16[128,2048]{1,0:T(8,128)(2,1)S(1)} collective-permute-done((bf16[128,2048]{1,0:T(8,128)(2,1)S(1)}, bf16[128,2048]{1,0:T(8,128)(2,1)S(1)}, u32[]{:S(2)}, u32[]{:S(2)}) %collective-permute-start.31) | collective-permute-done | bytes 524320 | tf_op jit(solution)/shard_map/ppermute | solution.py:312
  217.9 5.1 %shard_map.83 = (f32[128,2048]{1,0:T(8,128)S(1)}, bf16[128,2048]{1,0:T(8,128)(2,1)S(1)}) custom-call(s32[6]{0:T(128)S(1)} %pad_add_fusion.info_ref, bf16[512,512]{1,0:T(8,128)(2,1)S(1)} %shard_map.76.refs_0_, bf16[256,512]{1,0:T(8,128)(2,1)} %shard_map.81.refs_1_, bf16[512,512]{1,0:T(8,128)(2,1)S(1)} %collective-permute-done.14.refs_2_, ...), custom_call_target="tpu_custom_call" | custom-call | flops 4000000000 | tf_op jit(solution)/shard_map/pallas_call | solution.py:51
  223.2 5.0 %shard_map.80 = (f32[128,2048]{1,0:T(8,128)S(1)}, bf16[128,2048]{1,0:T(8,128)(2,1)S(1)}) custom-call(s32[6]{0:T(128)S(1)} %pad_add_fusion.info_ref, bf16[512,512]{1,0:T(8,128)(2,1)S(1)} %shard_map.76.refs_0_, bf16[256,512]{1,0:T(8,128)(2,1)S(1)} %shard_map.78.refs_1_, bf16[512,512]{1,0:T(8,128)(2,1)S(1)} %collective-permute-done.14.refs_2_, ...), custom_call_target="tpu_custom_call" | custom-call | flops 4000000000 | tf_op jit(solution)/shard_map/pallas_call | solution.py:51
  230.3 9.9 %collective-permute-done.32 = bf16[128,2048]{1,0:T(8,128)(2,1)S(1)} collective-permute-done((bf16[128,2048]{1,0:T(8,128)(2,1)S(1)}, bf16[128,2048]{1,0:T(8,128)(2,1)S(1)}, u32[]{:S(2)}, u32[]{:S(2)}) %collective-permute-start.32) | collective-permute-done | bytes 524320 | tf_op jit(solution)/shard_map/ppermute | solution.py:312
  240.4 10.2 %collective-permute-done.28 = bf16[128,2048]{1,0:T(8,128)(2,1)S(1)} collective-permute-done((bf16[128,2048]{1,0:T(8,128)(2,1)S(1)}, bf16[128,2048]{1,0:T(8,128)(2,1)S(1)}, u32[]{:S(2)}, u32[]{:S(2)}) %collective-permute-start.28) | collective-permute-done | bytes 524320 | tf_op jit(solution)/shard_map/ppermute | solution.py:312
  (119 shorter events, 52.4 us)
Async XLA Ops:
  6.5 80.5 %all-gather.5.cloned.1.call-start = ((), (), s32[]{:S(2)}) async-start(), calls=%async_computation | async-start | bytes 3145728 | tf_op jit(solution)/shard_map/all_gather | solution.py:349
  7.6 15.8 %collective-permute-start = (bf16[1024,256]{1,0:T(8,128)(2,1)S(1)}, bf16[1024,256]{1,0:T(8,128)(2,1)S(1)}, u32[]{:S(2)}, u32[]{:S(2)}) collective-permute-start(bf16[1024,256]{1,0:T(8,128)(2,1)S(1)} %dynamic-slice_bitcast_fusion.4), channel_id=1, source_target_pairs={{0,4},{4,0},{1,5},{5,1},{2,6},{6,2},{3,7},{7,3},{8,12},{12,8},{9,1... | collective-permute-start | bytes 1572872 | tf_op jit(solution)/shard_map/ppermute | solution.py:308
  13.8 130.1 %all-gather.7.cloned.1.call-start = ((), (), s32[]{:S(2)}) async-start(), calls=%async_computation.1 | async-start | bytes 3145728 | tf_op jit(solution)/shard_map/all_gather | solution.py:349
  16.9 31.7 %collective-permute-start.6 = (bf16[1024,512]{1,0:T(8,128)(2,1)}, bf16[1024,512]{1,0:T(8,128)(2,1)}, u32[]{:S(2)}, u32[]{:S(2)}) collective-permute-start(bf16[1024,512]{1,0:T(8,128)(2,1)} %get-tuple-element.70), channel_id=1, source_target_pairs={{0,4},{4,0},{1,5},{5,1},{2,6},{6,2},{3,7},{7,3},{8,12},{12,8},{9,1... | collective-permute-start | bytes 3145736 | tf_op jit(solution)/shard_map/ppermute | solution.py:308
  23.4 12.3 %collective-permute-start.1 = (bf16[1024,256]{1,0:T(8,128)(2,1)S(1)}, bf16[1024,256]{1,0:T(8,128)(2,1)S(1)}, u32[]{:S(2)}, u32[]{:S(2)}) collective-permute-start(bf16[1024,256]{1,0:T(8,128)(2,1)S(1)} %collective-permute-done.refs_0_), channel_id=1, source_target_pairs={{0,16},{8,24},{16,0},{24,8},{1,17},{9,25},{17,1},{25,9},{2,18},{10... | collective-permute-start | bytes 1572872 | tf_op jit(solution)/shard_map/ppermute | solution.py:312
  25.5 10.6 %collective-permute-start.2 = (bf16[1024,256]{1,0:T(8,128)(2,1)S(1)}, bf16[1024,256]{1,0:T(8,128)(2,1)S(1)}, u32[]{:S(2)}, u32[]{:S(2)}) collective-permute-start(bf16[1024,256]{1,0:T(8,128)(2,1)S(1)} %collective-permute-done.refs_0_), channel_id=1, source_target_pairs={{0,8},{8,0},{16,24},{24,16},{1,9},{9,1},{17,25},{25,17},{2,10},{10... | collective-permute-start | bytes 1572872 | tf_op jit(solution)/shard_map/ppermute | solution.py:312
  49.7 25.8 %collective-permute-start.8 = (bf16[1024,512]{1,0:T(8,128)(2,1)}, bf16[1024,512]{1,0:T(8,128)(2,1)}, u32[]{:S(2)}, u32[]{:S(2)}) collective-permute-start(bf16[1024,512]{1,0:T(8,128)(2,1)} %collective-permute-done.6.refs_0_), channel_id=1, source_target_pairs={{0,16},{8,24},{16,0},{24,8},{1,17},{9,25},{17,1},{25,9},{2,18},{10... | collective-permute-start | bytes 3145736 | tf_op jit(solution)/shard_map/ppermute | solution.py:312
  51.0 30.9 %collective-permute-start.4 = (bf16[1024,512]{1,0:T(8,128)(2,1)}, bf16[1024,512]{1,0:T(8,128)(2,1)}, u32[]{:S(2)}, u32[]{:S(2)}) collective-permute-start(bf16[1024,512]{1,0:T(8,128)(2,1)} %get-tuple-element.69), channel_id=1, source_target_pairs={{0,4},{4,0},{1,5},{5,1},{2,6},{6,2},{3,7},{7,3},{8,12},{12,8},{9,1... | collective-permute-start | bytes 3145736 | tf_op jit(solution)/shard_map/ppermute | solution.py:308
  52.5 35.8 %collective-permute-start.9 = (bf16[1024,512]{1,0:T(8,128)(2,1)}, bf16[1024,512]{1,0:T(8,128)(2,1)}, u32[]{:S(2)}, u32[]{:S(2)}) collective-permute-start(bf16[1024,512]{1,0:T(8,128)(2,1)} %collective-permute-done.6.refs_0_), channel_id=1, source_target_pairs={{0,8},{8,0},{16,24},{24,16},{1,9},{9,1},{17,25},{25,17},{2,10},{10... | collective-permute-start | bytes 3145736 | tf_op jit(solution)/shard_map/ppermute | solution.py:312
  75.5 12.9 %collective-permute-start.10 = (bf16[1024,512]{1,0:T(8,128)(2,1)}, bf16[1024,512]{1,0:T(8,128)(2,1)}, u32[]{:S(2)}, u32[]{:S(2)}) collective-permute-start(bf16[1024,512]{1,0:T(8,128)(2,1)} %collective-permute-done.8.refs_1_), channel_id=1, source_target_pairs={{0,8},{8,0},{16,24},{24,16},{1,9},{9,1},{17,25},{25,17},{2,10},{10... | collective-permute-start | bytes 3145736 | tf_op jit(solution)/shard_map/ppermute | solution.py:312
  75.6 8.7 %collective-permute-start.5 = (bf16[512,256]{1,0:T(8,128)(2,1)S(1)}, bf16[512,256]{1,0:T(8,128)(2,1)S(1)}, u32[]{:S(2)}, u32[]{:S(2)}) collective-permute-start(bf16[512,256]{1,0:T(8,128)(2,1)S(1)} %shard_map.74), channel_id=1, source_target_pairs={{0,16},{8,24},{16,0},{24,8},{1,17},{9,25},{17,1},{25,9},{2,18},{10... | collective-permute-start | bytes 786440 | tf_op jit(solution)/shard_map/ppermute | solution.py:312
  84.4 15.3 %collective-permute-start.11 = (bf16[1024,256]{1,0:T(8,128)(2,1)S(1)}, bf16[1024,256]{1,0:T(8,128)(2,1)}, u32[]{:S(2)}, u32[]{:S(2)}) collective-permute-start(bf16[1024,256]{1,0:T(8,128)(2,1)S(1)} %pad_maximum_fusion.1), channel_id=1, source_target_pairs={{0,4},{4,0},{1,5},{5,1},{2,6},{6,2},{3,7},{7,3},{8,12},{12,8},{9,1... | collective-permute-start | bytes 1572872 | tf_op jit(solution)/shard_map/ppermute | solution.py:308
  86.0 24.8 %collective-permute-start.15 = (bf16[1024,512]{1,0:T(8,128)(2,1)}, bf16[1024,512]{1,0:T(8,128)(2,1)}, u32[]{:S(2)}, u32[]{:S(2)}) collective-permute-start(bf16[1024,512]{1,0:T(8,128)(2,1)} %collective-permute-done.4.refs_0_), channel_id=1, source_target_pairs={{0,16},{8,24},{16,0},{24,8},{1,17},{9,25},{17,1},{25,9},{2,18},{10... | collective-permute-start | bytes 3145736 | tf_op jit(solution)/shard_map/ppermute | solution.py:312
  87.0 13.3 %collective-permute-start.12 = (bf16[512,256]{1,0:T(8,128)(2,1)S(1)}, bf16[512,256]{1,0:T(8,128)(2,1)}, u32[]{:S(2)}, u32[]{:S(2)}) collective-permute-start(bf16[512,256]{1,0:T(8,128)(2,1)S(1)} %collective-permute-done.5), channel_id=1, source_target_pairs={{0,8},{8,0},{16,24},{24,16},{1,9},{9,1},{17,25},{25,17},{2,10},{10... | collective-permute-start | bytes 786440 | tf_op jit(solution)/shard_map/ppermute | solution.py:312
  100.3 31.4 %collective-permute-start.16 = (bf16[1024,512]{1,0:T(8,128)(2,1)}, bf16[1024,512]{1,0:T(8,128)(2,1)}, u32[]{:S(2)}, u32[]{:S(2)}) collective-permute-start(bf16[1024,512]{1,0:T(8,128)(2,1)} %collective-permute-done.4.refs_0_), channel_id=1, source_target_pairs={{0,8},{8,0},{16,24},{24,16},{1,9},{9,1},{17,25},{25,17},{2,10},{10... | collective-permute-start | bytes 3145736 | tf_op jit(solution)/shard_map/ppermute | solution.py:312
  110.8 20.9 %collective-permute-start.17 = (bf16[1024,512]{1,0:T(8,128)(2,1)}, bf16[1024,512]{1,0:T(8,128)(2,1)}, u32[]{:S(2)}, u32[]{:S(2)}) collective-permute-start(bf16[1024,512]{1,0:T(8,128)(2,1)} %collective-permute-done.15.refs_1_), channel_id=1, source_target_pairs={{0,8},{8,0},{16,24},{24,16},{1,9},{9,1},{17,25},{25,17},{2,10},{10... | collective-permute-start | bytes 3145736 | tf_op jit(solution)/shard_map/ppermute | solution.py:312
  110.8 17.5 %collective-permute-start.14 = (bf16[512,512]{1,0:T(8,128)(2,1)S(1)}, bf16[512,512]{1,0:T(8,128)(2,1)S(1)}, u32[]{:S(2)}, u32[]{:S(2)}) collective-permute-start(bf16[512,512]{1,0:T(8,128)(2,1)S(1)} %shard_map.76.refs_0_), channel_id=1, source_target_pairs={{0,4},{4,0},{1,5},{5,1},{2,6},{6,2},{3,7},{7,3},{8,12},{12,8},{9,1... | collective-permute-start | bytes 1572872 | tf_op jit(solution)/shard_map/ppermute | solution.py:308
  116.1 43.8 %collective-permute-start.21 = (bf16[256,2048]{1,0:T(8,128)(2,1)S(1)}, bf16[256,2048]{1,0:T(8,128)(2,1)}, u32[]{:S(2)}, u32[]{:S(2)}) collective-permute-start(bf16[256,2048]{1,0:T(8,128)(2,1)S(1)} %dynamic-slice_bitcast_fusion.1.refs_6_), channel_id=1, source_target_pairs={{0,16},{8,24},{16,0},{24,8},{1,17},{9,25},{17,1},{25,9},{2,18},{10... | collective-permute-start | bytes 3145736 | tf_op jit(solution)/shard_map/ppermute | solution.py:312
  129.2 26.3 %collective-permute-start.19 = (bf16[512,512]{1,0:T(8,128)(2,1)}, bf16[512,512]{1,0:T(8,128)(2,1)}, u32[]{:S(2)}, u32[]{:S(2)}) collective-permute-start(bf16[512,512]{1,0:T(8,128)(2,1)} %broadcast_select_fusion), channel_id=1, source_target_pairs={{0,2},{1,3},{2,0},{3,1},{4,6},{5,7},{6,4},{7,5},{8,10},{9,11},{10,... | collective-permute-start | bytes 1572872 | tf_op jit(solution)/shard_map/ppermute | solution.py:312
  155.5 25.1 %collective-permute-start.25 = (bf16[256,2048]{1,0:T(8,128)(2,1)S(1)}, bf16[256,2048]{1,0:T(8,128)(2,1)}, u32[]{:S(2)}, u32[]{:S(2)}) collective-permute-start(bf16[256,2048]{1,0:T(8,128)(2,1)S(1)} %dynamic-slice_bitcast_fusion.refs_6_), channel_id=1, source_target_pairs={{0,16},{8,24},{16,0},{24,8},{1,17},{9,25},{17,1},{25,9},{2,18},{10... | collective-permute-start | bytes 3145736 | tf_op jit(solution)/shard_map/ppermute | solution.py:312
  160.0 33.8 %collective-permute-start.22 = (bf16[256,2048]{1,0:T(8,128)(2,1)S(1)}, bf16[256,2048]{1,0:T(8,128)(2,1)}, u32[]{:S(2)}, u32[]{:S(2)}) collective-permute-start(bf16[256,2048]{1,0:T(8,128)(2,1)S(1)} %dynamic-slice_bitcast_fusion.1.refs_6_), channel_id=1, source_target_pairs={{0,8},{8,0},{16,24},{24,16},{1,9},{9,1},{17,25},{25,17},{2,10},{10... | collective-permute-start | bytes 3145736 | tf_op jit(solution)/shard_map/ppermute | solution.py:312
  160.0 33.8 %collective-permute-start.23 = (bf16[256,2048]{1,0:T(8,128)(2,1)}, bf16[256,2048]{1,0:T(8,128)(2,1)}, u32[]{:S(2)}, u32[]{:S(2)}) collective-permute-start(bf16[256,2048]{1,0:T(8,128)(2,1)} %collective-permute-done.21.refs_7_), channel_id=1, source_target_pairs={{0,8},{8,0},{16,24},{24,16},{1,9},{9,1},{17,25},{25,17},{2,10},{10... | collective-permute-start | bytes 3145736 | tf_op jit(solution)/shard_map/ppermute | solution.py:312
  165.4 6.7 %collective-permute-start.29 = (bf16[256,512]{1,0:T(8,128)(2,1)}, bf16[256,512]{1,0:T(8,128)(2,1)}, u32[]{:S(2)}, u32[]{:S(2)}) collective-permute-start(bf16[256,512]{1,0:T(8,128)(2,1)} %shard_map.81.refs_1_), channel_id=1, source_target_pairs={{0,4},{4,0},{1,5},{5,1},{2,6},{6,2},{3,7},{7,3},{8,12},{12,8},{9,1... | collective-permute-start | bytes 786440 | tf_op jit(solution)/shard_map/ppermute | solution.py:308
  165.5 9.6 %collective-permute-start.18 = (bf16[256,512]{1,0:T(8,128)(2,1)S(1)}, bf16[256,512]{1,0:T(8,128)(2,1)S(1)}, u32[]{:S(2)}, u32[]{:S(2)}) collective-permute-start(bf16[256,512]{1,0:T(8,128)(2,1)S(1)} %shard_map.78.refs_1_), channel_id=1, source_target_pairs={{0,4},{4,0},{1,5},{5,1},{2,6},{6,2},{3,7},{7,3},{8,12},{12,8},{9,1... | collective-permute-start | bytes 786440 | tf_op jit(solution)/shard_map/ppermute | solution.py:308
  173.0 10.5 %collective-permute-start.30 = (bf16[256,512]{1,0:T(8,128)(2,1)S(1)}, bf16[256,512]{1,0:T(8,128)(2,1)S(1)}, u32[]{:S(2)}, u32[]{:S(2)}) collective-permute-start(bf16[256,512]{1,0:T(8,128)(2,1)S(1)} %broadcast_select_fusion.1), channel_id=1, source_target_pairs={{0,2},{1,3},{2,0},{3,1},{4,6},{5,7},{6,4},{7,5},{8,10},{9,11},{10,... | collective-permute-start | bytes 786440 | tf_op jit(solution)/shard_map/ppermute | solution.py:312
  175.1 42.8 %collective-permute-start.26 = (bf16[256,2048]{1,0:T(8,128)(2,1)S(1)}, bf16[256,2048]{1,0:T(8,128)(2,1)S(1)}, u32[]{:S(2)}, u32[]{:S(2)}) collective-permute-start(bf16[256,2048]{1,0:T(8,128)(2,1)S(1)} %dynamic-slice_bitcast_fusion.refs_6_), channel_id=1, source_target_pairs={{0,8},{8,0},{16,24},{24,16},{1,9},{9,1},{17,25},{25,17},{2,10},{10... | collective-permute-start | bytes 3145736 | tf_op jit(solution)/shard_map/ppermute | solution.py:312
  180.5 22.5 %collective-permute-start.20 = (bf16[256,512]{1,0:T(8,128)(2,1)S(1)}, bf16[256,512]{1,0:T(8,128)(2,1)S(1)}, u32[]{:S(2)}, u32[]{:S(2)}) collective-permute-start(bf16[256,512]{1,0:T(8,128)(2,1)S(1)} %broadcast_select_fusion.2), channel_id=1, source_target_pairs={{0,2},{1,3},{2,0},{3,1},{4,6},{5,7},{6,4},{7,5},{8,10},{9,11},{10,... | collective-permute-start | bytes 786440 | tf_op jit(solution)/shard_map/ppermute | solution.py:312
  183.5 34.4 %collective-permute-start.27 = (bf16[256,2048]{1,0:T(8,128)(2,1)}, bf16[256,2048]{1,0:T(8,128)(2,1)S(1)}, u32[]{:S(2)}, u32[]{:S(2)}) collective-permute-start(bf16[256,2048]{1,0:T(8,128)(2,1)} %collective-permute-done.25.refs_7_), channel_id=1, source_target_pairs={{0,8},{8,0},{16,24},{24,16},{1,9},{9,1},{17,25},{25,17},{2,10},{10... | collective-permute-start | bytes 3145736 | tf_op jit(solution)/shard_map/ppermute | solution.py:312
  202.9 14.9 %collective-permute-start.31 = (bf16[128,2048]{1,0:T(8,128)(2,1)S(1)}, bf16[128,2048]{1,0:T(8,128)(2,1)S(1)}, u32[]{:S(2)}, u32[]{:S(2)}) collective-permute-start(bf16[128,2048]{1,0:T(8,128)(2,1)S(1)} %get-tuple-element.66), channel_id=1, source_target_pairs={{0,1},{1,0},{2,3},{3,2},{4,5},{5,4},{6,7},{7,6},{8,9},{9,8},{10,11... | collective-permute-start | bytes 1572872 | tf_op jit(solution)/shard_map/ppermute | solution.py:312
  208.6 21.6 %collective-permute-start.24 = (bf16[128,2048]{1,0:T(8,128)(2,1)S(1)}, bf16[128,2048]{1,0:T(8,128)(2,1)S(1)}, u32[]{:S(2)}, u32[]{:S(2)}) collective-permute-start(bf16[128,2048]{1,0:T(8,128)(2,1)S(1)} %get-tuple-element.57), channel_id=1, source_target_pairs={{0,1},{1,0},{2,3},{3,2},{4,5},{5,4},{6,7},{7,6},{8,9},{9,8},{10,11... | collective-permute-start | bytes 1572872 | tf_op jit(solution)/shard_map/ppermute | solution.py:312
  223.1 17.2 %collective-permute-start.32 = (bf16[128,2048]{1,0:T(8,128)(2,1)S(1)}, bf16[128,2048]{1,0:T(8,128)(2,1)S(1)}, u32[]{:S(2)}, u32[]{:S(2)}) collective-permute-start(bf16[128,2048]{1,0:T(8,128)(2,1)S(1)} %get-tuple-element.68), channel_id=1, source_target_pairs={{0,1},{1,0},{2,3},{3,2},{4,5},{5,4},{6,7},{7,6},{8,9},{9,8},{10,11... | collective-permute-start | bytes 1572872 | tf_op jit(solution)/shard_map/ppermute | solution.py:312
  228.1 22.4 %collective-permute-start.28 = (bf16[128,2048]{1,0:T(8,128)(2,1)S(1)}, bf16[128,2048]{1,0:T(8,128)(2,1)S(1)}, u32[]{:S(2)}, u32[]{:S(2)}) collective-permute-start(bf16[128,2048]{1,0:T(8,128)(2,1)S(1)} %get-tuple-element.63), channel_id=1, source_target_pairs={{0,1},{1,0},{2,3},{3,2},{4,5},{5,4},{6,7},{7,6},{8,9},{9,8},{10,11... | collective-permute-start | bytes 1572872 | tf_op jit(solution)/shard_map/ppermute | solution.py:312
  (20 other events, 101.6 us)
Sparse Core Ops, SparseCore 0:
  13.9 56.8 all-gather.4
  75.6 57.7 all-gather.6
where the time goes:
time: 262 us; the launch traced here: 259 us
  waiting for transfers between devices  85.6 us (33%)
  Pallas kernels  65.6 us (25%)
  starting transfers between devices  49.3 us (19%)
  local copies, waits for them, and re-layouts  32.3 us (12%)
  between operations  17 us (6%)
  other arithmetic  9.19 us (4%)
    pallas_call x11, Pallas kernels, call(): pl.pallas_call(kernel, in_specs=specs, out_specs=[VMEM] * len(shapes), ou...  65.6 us
    ppermute x26, waiting for transfers between devices, swap(): return lax.ppermute(array, name, [(i, i ^ bit) for i in range(4)])  62.9 us
    ppermute x26, starting transfers between devices, swap(): return lax.ppermute(array, name, [(i, i ^ bit) for i in range(4)])  35.8 us
    ppermute x7, waiting for transfers between devices, swap_uly(): return lax.ppermute(array, 'uly', [(0, 1), (1, 0)])  22.6 us
    unnamed x36, local copies, waits for them, and re-layouts  21.8 us
    ppermute x7, starting transfers between devices, swap_uly(): return lax.ppermute(array, 'uly', [(0, 1), (1, 0)])  13.5 us
  transfers between devices with their start and end apart: 35, of which 15 were waited for; matrix products, arithmetic and copies ran while one was open for 7% of the time, Pallas kernels for 25%

commit v1 on v0

--- a/solution.py
+++ b/solution.py
@@ -106,29 +106,34 @@
 
 def proj_kernel(first_column, rotated, own_ref, rest_ref, *refs):
     pieces, refs = refs[:4], refs[4:]
-    weights_ref, cos_ref, sin_ref, out_ref, scratch, sems = refs
+    weights_ref, cos_ref, sin_ref, out_ref, own, rest, scratch, sems = refs
     depth, columns = scratch.shape
-    part = depth // 4
-    copies = [
+    run = depth // 4
+    parts = [slice(i * run, (i + 1) * run) for i in range(4)]
+    rest_copies = [
+        pltpu.make_async_copy(rest_ref.at[:, p], rest.at[:, p], sems.at[i])
+        for i, p in enumerate(parts)
+    ]
+    own_copies = [
+        pltpu.make_async_copy(own_ref.at[:, p], own.at[:, p], sems.at[4 + i])
+        for i, p in enumerate(parts)
+    ]
+    weight_copies = [
         pltpu.make_async_copy(
-            weights_ref.at[pl.ds(i * part, part), pl.ds(first_column, columns)],
-            scratch.at[pl.ds(i * part, part)],
-            sems.at[i],
+            weights_ref.at[p, pl.ds(first_column, columns)], scratch.at[p], sems.at[8 + i]
         )
-        for i in range(4)
+        for i, p in enumerate(parts)
     ]
-    for copy in copies:
+    for copy in (*rest_copies, *weight_copies, *own_copies):
         copy.start()
     total = None
     for i, piece in enumerate(pieces):
-        run = piece.shape[0]
-        product = jnp.dot(
-            rest_ref[:, i * run : (i + 1) * run], piece[...], preferred_element_type=jnp.float32
-        )
+        rest_copies[i].wait()
+        product = jnp.dot(rest[:, parts[i]], piece[...], preferred_element_type=jnp.float32)
         total = product if total is None else total + product
-    for copy in copies:
+    for copy in (*weight_copies, *own_copies):
         copy.wait()
-    total += jnp.dot(own_ref[...], scratch[...], preferred_element_type=jnp.float32)
+    total += jnp.dot(own[...], scratch[...], preferred_element_type=jnp.float32)
     for i in range(columns // HEAD_SIZE):
         lanes = slice(i * HEAD_SIZE, (i + 1) * HEAD_SIZE)
         head = total[:, lanes]
@@ -142,12 +147,17 @@
     columns = pieces[0].shape[1]
     return call(
         functools.partial(proj_kernel, first_column, rotated),
-        [*[VMEM] * 6, HBM, VMEM, VMEM],
+        [HBM, HBM, *[VMEM] * 4, HBM, VMEM, VMEM],
         [((rows, columns), jnp.bfloat16)],
         (own, rest, *pieces, weights, *tables),
         COST[cost],
-        [pltpu.VMEM((weights.shape[0], columns), jnp.bfloat16), pltpu.SemaphoreType.DMA((4,))],
-        vmem=40,
+        [
+            pltpu.VMEM(own.shape, jnp.bfloat16),
+            pltpu.VMEM(rest.shape, jnp.bfloat16),
+            pltpu.VMEM((weights.shape[0], columns), jnp.bfloat16),
+            pltpu.SemaphoreType.DMA((12,)),
+        ],
+        vmem=44,
     )[0]
 
 
@@ -388,7 +398,6 @@
     info = jnp.concatenate([jnp.stack([my_block, first_key[0] // BLOCK]), slot_of_block])
     first_key = first_key[None, :]
 
-
     w0_z = other(after(w0_both, pair))
     a_y = after(a_y, pair_c)
     a_yx = along(a_y)
@@ -399,7 +408,7 @@
     b_y = after(b_y, pair_x)
     b_yx = along(b_y)
     queries_a = project(
-        "queries_a", own, after(rest, b_y, w0_z), pieces, weights, 0, 4, tables
+        "queries_a", own, after(rest, w0_z), pieces, weights, 0, 4, tables
     )
     two_y = after(two_y, queries_a)
     pairs = (
@@ -422,7 +431,7 @@
     quarter = BLOCK // 4
     halves = [((h * quarter, quarter), ((2 + h) * quarter, quarter)) for h in range(2)]
     att_b, att_b_y, far_b = [], [], []
-    ready = after(info, att_a_y, *([w1_z] if 1==2 else []))
+    ready = after(info, att_a_y)
     for h in range(2):
         att_b.append(attend(f"att_b{h}", ready, queries_b, pairs, first_key, 0, 4, halves[h]))
         att_b_y.append(swap_uly(att_b[h]))
@@ -433,7 +442,7 @@
     w1_z = after(w1_z, att_b[0])
     w1_zx = along(w1_z)
 
-    late = queries_b
+    late = sent
     w_quarters = [
         [w0_z, w0_zx, across(after(w0_z, late)), across(after(w0_zx, late))],
         [w1_z, w1_zx, across(after(w1_z, late)), across(after(w1_zx, late))],

time: 262 us -> 263 us (level)
  waiting for transfers between devices: 85.6 us -> 99.2 us
  starting transfers between devices: 49.3 us -> 36.8 us
  local copies, waits for them, and re-layouts: 32.3 us -> 26.4 us
  Pallas kernels: 65.6 us -> 68.6 us
    ppermute x26, starting transfers between devices: 35.8 us -> 23.2 us  [swap(): return lax.ppermute(array, name, [(i, i ^ bit) for i in range(4)])]
    all_gather x2, waiting for transfers between devices: 0.01 us -> 8.1 us  [two_along_tp(): lax.all_gather(piece, 'tp', axis=0, axis_index_groups=[[0, 2], [1, 3]])]
    ppermute x26, waiting for transfers between devices: 62.9 us -> 68.6 us  [swap(): return lax.ppermute(array, name, [(i, i ^ bit) for i in range(4)])]
    unnamed x36 -> x42, local copies, waits for them, and re-layouts: 21.8 us -> 17.1 us
    pallas_call x11, Pallas kernels: 65.6 us -> 68.6 us  [call(): pl.pallas_call(kernel, in_specs=specs, out_specs=[VMEM] * len(shapes), ou...]
  transfers between devices with their start and end apart: 35 -> 35, of which waited for: 15 -> 17; matrix products, arithmetic and copies ran while one was open for 7% -> 7% of each run, Pallas kernels for 25% -> 27%
where the time goes in v1:
time: 263 us; the launch traced here: 258 us
  waiting for transfers between devices  99.2 us (38%)
  Pallas kernels  68.6 us (26%)
  starting transfers between devices  36.8 us (14%)
  local copies, waits for them, and re-layouts  26.4 us (10%)
  between operations  17.2 us (7%)
  other arithmetic  9.92 us (4%)
    pallas_call x11, Pallas kernels, call(): pl.pallas_call(kernel, in_specs=specs, out_specs=[VMEM] * len(shapes), ou...  68.6 us
    ppermute x26, waiting for transfers between devices, swap(): return lax.ppermute(array, name, [(i, i ^ bit) for i in range(4)])  68.6 us
    ppermute x26, starting transfers between devices, swap(): return lax.ppermute(array, name, [(i, i ^ bit) for i in range(4)])  23.2 us
    ppermute x7, waiting for transfers between devices, swap_uly(): return lax.ppermute(array, 'uly', [(0, 1), (1, 0)])  22.5 us
    unnamed x42, local copies, waits for them, and re-layouts  17.1 us
    ppermute x7, starting transfers between devices, swap_uly(): return lax.ppermute(array, 'uly', [(0, 1), (1, 0)])  13.5 us
    all_gather x2, waiting for transfers between devices, two_along_tp(): lax.all_gather(piece, 'tp', axis=0, axis_index_groups=[[0, 2], [1, 3]])  8.1 us
  transfers between devices with their start and end apart: 35, of which 17 were waited for; matrix products, arithmetic and copies ran while one was open for 7% of the time, Pallas kernels for 27%

profile of v1, /device:TPU:0, one launch (start us, length us, event | category | flops | bytes accessed | tf_op | source)
XLA Modules:
  0.0 258.1 jit_solution(7440046418083999694)
XLA Ops:
  7.6 3.0 %collective-permute-start = (bf16[1024,256]{1,0:T(8,128)(2,1)S(1)}, bf16[1024,256]{1,0:T(8,128)(2,1)S(1)}, u32[]{:S(2)}, u32[]{:S(2)}) collective-permute-start(bf16[1024,256]{1,0:T(8,128)(2,1)S(1)} %dynamic-slice_bitcast_fusion.4), channel_id=1, source_target_pairs={{0,4},{4,0},{1,5},{5,1},{2,6},{6,2},{3,7},{7,3},{8,12},{12,8},{9,1... | collective-permute-start | bytes 1572872 | tf_op jit(solution)/shard_map/ppermute | solution.py:318
  10.7 3.1 %constant_dynamic-slice_fusion.1 = (bf16[256,2048]{1,0:T(8,128)(2,1)}, bf16[256,2048]{1,0:T(8,128)(2,1)}) fusion(bf16[1024,4096]{1,0:T(8,128)(2,1)} %refs_10_.7, s32[]{:T(128)S(6)} %select_n.82), kind=kLoop, calls=%fused_computation.40 | loop fusion | bytes 4194308 | tf_op jit(solution)/shard_map/dynamic_slice | solution.py:345
  13.9 3.0 %dynamic-slice_bitcast_fusion.2 = (bf16[1024,512]{1,0:T(8,128)(2,1)}, bf16[1024,512]{1,0:T(8,128)(2,1)}) fusion(bf16[4096,1,1280]{2,0,1:T(8,128)(2,1)} %param.9, s32[]{:T(128)S(6)} %select_n.81), kind=kLoop, calls=%fused_computation.9 | loop fusion | bytes 4194308 | tf_op jit(solution)/shard_map/dynamic_slice | solution.py:342
  19.5 3.9 %collective-permute-done.refs_0_ = bf16[1024,256]{1,0:T(8,128)(2,1)S(1)} collective-permute-done((bf16[1024,256]{1,0:T(8,128)(2,1)S(1)}, bf16[1024,256]{1,0:T(8,128)(2,1)S(1)}, u32[]{:S(2)}, u32[]{:S(2)}) %collective-permute-start) | collective-permute-done | bytes 524320 | tf_op jit(solution)/shard_map/ppermute | solution.py:318
  25.6 10.0 %shard_map.73 = (bf16[512,4096]{1,0:T(8,128)(2,1)}, bf16[512,4096]{1,0:T(8,128)(2,1)}) custom-call(s32[5]{0:T(128)S(1)} %pad_add_fusion.1.start_ref, bf16[512,8192]{1,0:T(8,128)(2,1)} %hidden_ref, bf16[1,8192]{1,0:T(2,128)(2,1)S(1)} %reshape.41.gain_ref), custom_call_target="tpu_custom_call" | custom-call | flops 4000000000 | tf_op jit(solution)/shard_map/pallas_call | solution.py:51
  37.7 2.2 copy-done.1
  39.9 6.4 %shard_map.74 = bf16[512,256]{1,0:T(8,128)(2,1)S(1)} custom-call(bf16[512,4096]{1,0:T(8,128)(2,1)S(1)} %copy-done.1, bf16[512,4096]{1,0:T(8,128)(2,1)} %get-tuple-element.50.rest_ref, bf16[1024,256]{1,0:T(8,128)(2,1)S(1)} %collective-permute-done.refs_0_, bf16[1024,256]{1,0:T(8,128)(2,1)S(1)} %collective-permute-done.1.refs_1_, ...), custom_call_target="tpu_custom_call" | custom-call | flops 1000000000 | tf_op jit(solution)/shard_map/pallas_call | solution.py:51
  50.7 23.0 %collective-permute-done.6.refs_1_ = bf16[1024,512]{1,0:T(8,128)(2,1)} collective-permute-done((bf16[1024,512]{1,0:T(8,128)(2,1)}, bf16[1024,512]{1,0:T(8,128)(2,1)}, u32[]{:S(2)}, u32[]{:S(2)}) %collective-permute-start.6) | collective-permute-done | bytes 1048608 | tf_op jit(solution)/shard_map/ppermute | solution.py:322
  79.7 2.9 %collective-permute-done.9 = bf16[512,256]{1,0:T(8,128)(2,1)S(1)} collective-permute-done((bf16[512,256]{1,0:T(8,128)(2,1)S(1)}, bf16[512,256]{1,0:T(8,128)(2,1)S(1)}, u32[]{:S(2)}, u32[]{:S(2)}) %collective-permute-start.9) | collective-permute-done | bytes 262176 | tf_op jit(solution)/shard_map/ppermute | solution.py:322
  88.8 8.7 %shard_map.75.q_ref = bf16[512,512]{1,0:T(8,128)(2,1)S(1)} custom-call(bf16[512,4096]{1,0:T(8,128)(2,1)S(1)} %copy-done.2, bf16[512,4096]{1,0:T(8,128)(2,1)} %get-tuple-element.50.rest_ref, bf16[1024,512]{1,0:T(8,128)(2,1)} %collective-permute-done.4.refs_0_, bf16[1024,512]{1,0:T(8,128)(2,1)} %collective-permute-done.6.refs_1_, ...), custom_call_target="tpu_custom_call" | custom-call | flops 4000000000 | tf_op jit(solution)/shard_map/pallas_call | solution.py:51
  100.3 5.1 %shard_map.76.refs_0_ = bf16[512,512]{1,0:T(8,128)(2,1)S(1)} custom-call(s32[10]{0:T(128)S(1)} %pad_add_fusion.2.info_ref, bf16[512,512]{1,0:T(8,128)(2,1)S(1)} %shard_map.75.q_ref, s32[1,512]{1,0:T(1,128)S(1)} %bitcast.28, bf16[2048,256]{1,0:T(8,128)(2,1)S(1)} %pad_maximum_fusion.refs_0_, bf16[2048,256]{1,0:T(8,128)(2,1)S(1)} %constant_dynamic-update-slice_fusion.refs_1_), custom_call_target="tpu_custom_call" | custom-call | flops 4000000000 | tf_op jit(solution)/shard_map/pallas_call | solution.py:51
  105.4 3.6 %collective-permute-done.15.refs_1_ = bf16[1024,512]{1,0:T(8,128)(2,1)} collective-permute-done((bf16[1024,512]{1,0:T(8,128)(2,1)}, bf16[1024,512]{1,0:T(8,128)(2,1)}, u32[]{:S(2)}, u32[]{:S(2)}) %collective-permute-start.15) | collective-permute-done | bytes 1048608 | tf_op jit(solution)/shard_map/ppermute | solution.py:322
  109.5 5.4 %collective-permute-start.21 = (bf16[256,2048]{1,0:T(8,128)(2,1)S(1)}, bf16[256,2048]{1,0:T(8,128)(2,1)}, u32[]{:S(2)}, u32[]{:S(2)}) collective-permute-start(bf16[256,2048]{1,0:T(8,128)(2,1)S(1)} %dynamic-slice_bitcast_fusion.1.refs_6_), channel_id=1, source_target_pairs={{0,16},{8,24},{16,0},{24,8},{1,17},{9,25},{17,1},{25,9},{2,18},{10... | collective-permute-start | bytes 3145736 | tf_op jit(solution)/shard_map/ppermute | solution.py:322
  114.9 8.4 %collective-permute-done.13.refs_2_ = bf16[512,512]{1,0:T(8,128)(2,1)S(1)} collective-permute-done((bf16[512,512]{1,0:T(8,128)(2,1)S(1)}, bf16[512,512]{1,0:T(8,128)(2,1)S(1)}, u32[]{:S(2)}, u32[]{:S(2)}) %collective-permute-start.13) | collective-permute-done | bytes 524320 | tf_op jit(solution)/shard_map/ppermute | solution.py:318
  124.2 2.6 %collective-permute-start.19 = (bf16[512,512]{1,0:T(8,128)(2,1)}, bf16[512,512]{1,0:T(8,128)(2,1)}, u32[]{:S(2)}, u32[]{:S(2)}) collective-permute-start(bf16[512,512]{1,0:T(8,128)(2,1)} %broadcast_select_fusion), channel_id=1, source_target_pairs={{0,2},{1,3},{2,0},{3,1},{4,6},{5,7},{6,4},{7,5},{8,10},{9,11},{10,... | collective-permute-start | bytes 1572872 | tf_op jit(solution)/shard_map/ppermute | solution.py:322
  126.8 2.2 copy-done.3
  129.0 8.7 %shard_map.77.q_ref = bf16[512,512]{1,0:T(8,128)(2,1)S(1)} custom-call(bf16[512,4096]{1,0:T(8,128)(2,1)S(1)} %copy-done.3, bf16[512,4096]{1,0:T(8,128)(2,1)} %get-tuple-element.50.rest_ref, bf16[1024,512]{1,0:T(8,128)(2,1)} %collective-permute-done.14.refs_0_, bf16[1024,512]{1,0:T(8,128)(2,1)} %collective-permute-done.15.refs_1_, ...), custom_call_target="tpu_custom_call" | custom-call | flops 1000000 | tf_op jit(solution)/shard_map/pallas_call | solution.py:51
  137.7 8.1 %all-gather.7.cloned.1.call-done = bf16[512,2048]{1,0:T(8,128)(2,1)} async-done(((bf16[256,2048]{1,0:T(8,128)(2,1)}), bf16[512,2048]{1,0:T(8,128)(2,1)}) %all-gather.7.cloned.1.call-update) | async-done | bytes 2097168 | tf_op jit(solution)/shard_map/all_gather | solution.py:359
  148.3 4.0 %shard_map.78.refs_1_ = bf16[256,512]{1,0:T(8,128)(2,1)S(1)} custom-call(s32[10]{0:T(128)S(1)} %pad_add_fusion.2.info_ref, bf16[512,512]{1,0:T(8,128)(2,1)S(1)} %shard_map.77.q_ref, s32[1,512]{1,0:T(1,128)S(1)} %bitcast.29, bf16[2048,256]{1,0:T(8,128)(2,1)S(1)} %copy-done.10, bf16[2048,256]{1,0:T(8,128)(2,1)S(1)} %copy-done.14), custom_call_target="tpu_custom_call" | custom-call | flops 4000000000 | tf_op jit(solution)/shard_map/pallas_call | solution.py:51
  154.7 4.2 %shard_map.79.refs_1_ = bf16[256,512]{1,0:T(8,128)(2,1)S(1)} custom-call(s32[10]{0:T(128)S(1)} %pad_add_fusion.2.info_ref, bf16[512,512]{1,0:T(8,128)(2,1)S(1)} %copy-done.12, s32[1,512]{1,0:T(1,128)S(1)} %bitcast.30, bf16[2048,256]{1,0:T(8,128)(2,1)S(1)} %copy-done.10, bf16[2048,256]{1,0:T(8,128)(2,1)S(1)} %copy-done.14), custom_call_target="tpu_custom_call" | custom-call | flops 4000000000 | tf_op jit(solution)/shard_map/pallas_call | solution.py:51
  158.9 5.7 %collective-permute-start.22 = (bf16[256,512]{1,0:T(8,128)(2,1)S(1)}, bf16[256,512]{1,0:T(8,128)(2,1)S(1)}, u32[]{:S(2)}, u32[]{:S(2)}) collective-permute-start(bf16[256,512]{1,0:T(8,128)(2,1)S(1)} %shard_map.79.refs_1_), channel_id=1, source_target_pairs={{0,4},{4,0},{1,5},{5,1},{2,6},{6,2},{3,7},{7,3},{8,12},{12,8},{9,1... | collective-permute-start | bytes 786440 | tf_op jit(solution)/shard_map/ppermute | solution.py:318
  166.7 3.1 %collective-permute-done.22.refs_3_ = bf16[256,512]{1,0:T(8,128)(2,1)S(1)} collective-permute-done((bf16[256,512]{1,0:T(8,128)(2,1)S(1)}, bf16[256,512]{1,0:T(8,128)(2,1)S(1)}, u32[]{:S(2)}, u32[]{:S(2)}) %collective-permute-start.22) | collective-permute-done | bytes 262176 | tf_op jit(solution)/shard_map/ppermute | solution.py:318
  172.4 7.1 %collective-permute-done.18.refs_3_ = bf16[256,512]{1,0:T(8,128)(2,1)} collective-permute-done((bf16[256,512]{1,0:T(8,128)(2,1)S(1)}, bf16[256,512]{1,0:T(8,128)(2,1)}, u32[]{:S(2)}, u32[]{:S(2)}) %collective-permute-start.18) | collective-permute-done | bytes 262176 | tf_op jit(solution)/shard_map/ppermute | solution.py:318
  180.5 8.2 %collective-permute-done.26.refs_7_ = bf16[256,2048]{1,0:T(8,128)(2,1)} collective-permute-done((bf16[256,2048]{1,0:T(8,128)(2,1)S(1)}, bf16[256,2048]{1,0:T(8,128)(2,1)}, u32[]{:S(2)}, u32[]{:S(2)}) %collective-permute-start.26) | collective-permute-done | bytes 1048608 | tf_op jit(solution)/shard_map/ppermute | solution.py:322
  190.7 3.4 %copy-done = bf16[1024,4096]{1,0:T(8,128)(2,1)S(1)} copy-done((bf16[1024,4096]{1,0:T(8,128)(2,1)S(1)}, bf16[1024,4096]{1,0:T(8,128)(2,1)}, u32[]{:S(2)}) %copy-start) | copy-done | bytes 8388632
  195.9 5.6 %shard_map.82 = (f32[128,2048]{1,0:T(8,128)S(1)}, bf16[128,2048]{1,0:T(8,128)(2,1)S(1)}) custom-call(s32[6]{0:T(128)S(1)} %pad_add_fusion.info_ref, bf16[512,512]{1,0:T(8,128)(2,1)S(1)} %shard_map.76.refs_0_, bf16[256,512]{1,0:T(8,128)(2,1)S(1)} %copy-done.5, bf16[512,512]{1,0:T(8,128)(2,1)S(1)} %collective-permute-done.13.refs_2_, ...), custom_call_target="tpu_custom_call" | custom-call | flops 4000000000 | tf_op jit(solution)/shard_map/pallas_call | solution.py:51
  203.7 5.9 %shard_map.80 = (f32[128,2048]{1,0:T(8,128)S(1)}, bf16[128,2048]{1,0:T(8,128)(2,1)S(1)}) custom-call(s32[6]{0:T(128)S(1)} %pad_add_fusion.info_ref, bf16[512,512]{1,0:T(8,128)(2,1)S(1)} %shard_map.76.refs_0_, bf16[256,512]{1,0:T(8,128)(2,1)S(1)} %shard_map.78.refs_1_, bf16[512,512]{1,0:T(8,128)(2,1)S(1)} %collective-permute-done.13.refs_2_, ...), custom_call_target="tpu_custom_call" | custom-call | flops 4000000000 | tf_op jit(solution)/shard_map/pallas_call | solution.py:51
  209.7 6.7 %collective-permute-done.31 = bf16[128,2048]{1,0:T(8,128)(2,1)S(1)} collective-permute-done((bf16[128,2048]{1,0:T(8,128)(2,1)S(1)}, bf16[128,2048]{1,0:T(8,128)(2,1)S(1)}, u32[]{:S(2)}, u32[]{:S(2)}) %collective-permute-start.31) | collective-permute-done | bytes 524320 | tf_op jit(solution)/shard_map/ppermute | solution.py:322
  216.6 5.0 %shard_map.83 = (f32[128,2048]{1,0:T(8,128)S(1)}, bf16[128,2048]{1,0:T(8,128)(2,1)S(1)}) custom-call(s32[6]{0:T(128)S(1)} %pad_add_fusion.info_ref, bf16[512,512]{1,0:T(8,128)(2,1)S(1)} %shard_map.76.refs_0_, bf16[256,512]{1,0:T(8,128)(2,1)S(1)} %copy-done.5, bf16[512,512]{1,0:T(8,128)(2,1)S(1)} %collective-permute-done.13.refs_2_, ...), custom_call_target="tpu_custom_call" | custom-call | flops 4000000000 | tf_op jit(solution)/shard_map/pallas_call | solution.py:51
  222.9 5.0 %shard_map.81 = (f32[128,2048]{1,0:T(8,128)S(1)}, bf16[128,2048]{1,0:T(8,128)(2,1)S(1)}) custom-call(s32[6]{0:T(128)S(1)} %pad_add_fusion.info_ref, bf16[512,512]{1,0:T(8,128)(2,1)S(1)} %shard_map.76.refs_0_, bf16[256,512]{1,0:T(8,128)(2,1)S(1)} %shard_map.78.refs_1_, bf16[512,512]{1,0:T(8,128)(2,1)S(1)} %collective-permute-done.13.refs_2_, ...), custom_call_target="tpu_custom_call" | custom-call | flops 4000000000 | tf_op jit(solution)/shard_map/pallas_call | solution.py:51
  228.9 10.0 %collective-permute-done.32 = bf16[128,2048]{1,0:T(8,128)(2,1)S(1)} collective-permute-done((bf16[128,2048]{1,0:T(8,128)(2,1)S(1)}, bf16[128,2048]{1,0:T(8,128)(2,1)S(1)}, u32[]{:S(2)}, u32[]{:S(2)}) %collective-permute-start.32) | collective-permute-done | bytes 524320 | tf_op jit(solution)/shard_map/ppermute | solution.py:322
  239.0 10.2 %collective-permute-done.29 = bf16[128,2048]{1,0:T(8,128)(2,1)S(1)} collective-permute-done((bf16[128,2048]{1,0:T(8,128)(2,1)S(1)}, bf16[128,2048]{1,0:T(8,128)(2,1)S(1)}, u32[]{:S(2)}, u32[]{:S(2)}) %collective-permute-start.29) | collective-permute-done | bytes 524320 | tf_op jit(solution)/shard_map/ppermute | solution.py:322
  (125 shorter events, 46.6 us)
Async XLA Ops:
  6.5 78.7 %all-gather.5.cloned.1.call-start = ((), (), s32[]{:S(2)}) async-start(), calls=%async_computation | async-start | bytes 3145728 | tf_op jit(solution)/shard_map/all_gather | solution.py:359
  7.6 15.8 %collective-permute-start = (bf16[1024,256]{1,0:T(8,128)(2,1)S(1)}, bf16[1024,256]{1,0:T(8,128)(2,1)S(1)}, u32[]{:S(2)}, u32[]{:S(2)}) collective-permute-start(bf16[1024,256]{1,0:T(8,128)(2,1)S(1)} %dynamic-slice_bitcast_fusion.4), channel_id=1, source_target_pairs={{0,4},{4,0},{1,5},{5,1},{2,6},{6,2},{3,7},{7,3},{8,12},{12,8},{9,1... | collective-permute-start | bytes 1572872 | tf_op jit(solution)/shard_map/ppermute | solution.py:318
  13.8 132.0 %all-gather.7.cloned.1.call-start = ((), (), s32[]{:S(2)}) async-start(), calls=%async_computation.1 | async-start | bytes 3145728 | tf_op jit(solution)/shard_map/all_gather | solution.py:359
  16.9 29.9 %collective-permute-start.4 = (bf16[1024,512]{1,0:T(8,128)(2,1)}, bf16[1024,512]{1,0:T(8,128)(2,1)}, u32[]{:S(2)}, u32[]{:S(2)}) collective-permute-start(bf16[1024,512]{1,0:T(8,128)(2,1)} %get-tuple-element.70), channel_id=1, source_target_pairs={{0,4},{4,0},{1,5},{5,1},{2,6},{6,2},{3,7},{7,3},{8,12},{12,8},{9,1... | collective-permute-start | bytes 3145736 | tf_op jit(solution)/shard_map/ppermute | solution.py:318
  23.4 12.3 %collective-permute-start.1 = (bf16[1024,256]{1,0:T(8,128)(2,1)S(1)}, bf16[1024,256]{1,0:T(8,128)(2,1)S(1)}, u32[]{:S(2)}, u32[]{:S(2)}) collective-permute-start(bf16[1024,256]{1,0:T(8,128)(2,1)S(1)} %collective-permute-done.refs_0_), channel_id=1, source_target_pairs={{0,16},{8,24},{16,0},{24,8},{1,17},{9,25},{17,1},{25,9},{2,18},{10... | collective-permute-start | bytes 1572872 | tf_op jit(solution)/shard_map/ppermute | solution.py:322
  25.5 10.6 %collective-permute-start.2 = (bf16[1024,256]{1,0:T(8,128)(2,1)S(1)}, bf16[1024,256]{1,0:T(8,128)(2,1)S(1)}, u32[]{:S(2)}, u32[]{:S(2)}) collective-permute-start(bf16[1024,256]{1,0:T(8,128)(2,1)S(1)} %collective-permute-done.refs_0_), channel_id=1, source_target_pairs={{0,8},{8,0},{16,24},{24,16},{1,9},{9,1},{17,25},{25,17},{2,10},{10... | collective-permute-start | bytes 1572872 | tf_op jit(solution)/shard_map/ppermute | solution.py:322
  47.9 25.8 %collective-permute-start.6 = (bf16[1024,512]{1,0:T(8,128)(2,1)}, bf16[1024,512]{1,0:T(8,128)(2,1)}, u32[]{:S(2)}, u32[]{:S(2)}) collective-permute-start(bf16[1024,512]{1,0:T(8,128)(2,1)} %collective-permute-done.4.refs_0_), channel_id=1, source_target_pairs={{0,16},{8,24},{16,0},{24,8},{1,17},{9,25},{17,1},{25,9},{2,18},{10... | collective-permute-start | bytes 3145736 | tf_op jit(solution)/shard_map/ppermute | solution.py:322
  49.2 35.0 %collective-permute-start.14 = (bf16[1024,512]{1,0:T(8,128)(2,1)}, bf16[1024,512]{1,0:T(8,128)(2,1)}, u32[]{:S(2)}, u32[]{:S(2)}) collective-permute-start(bf16[1024,512]{1,0:T(8,128)(2,1)} %get-tuple-element.69), channel_id=1, source_target_pairs={{0,4},{4,0},{1,5},{5,1},{2,6},{6,2},{3,7},{7,3},{8,12},{12,8},{9,1... | collective-permute-start | bytes 3145736 | tf_op jit(solution)/shard_map/ppermute | solution.py:318
  50.7 35.8 %collective-permute-start.7 = (bf16[1024,512]{1,0:T(8,128)(2,1)}, bf16[1024,512]{1,0:T(8,128)(2,1)}, u32[]{:S(2)}, u32[]{:S(2)}) collective-permute-start(bf16[1024,512]{1,0:T(8,128)(2,1)} %collective-permute-done.4.refs_0_), channel_id=1, source_target_pairs={{0,8},{8,0},{16,24},{24,16},{1,9},{9,1},{17,25},{25,17},{2,10},{10... | collective-permute-start | bytes 3145736 | tf_op jit(solution)/shard_map/ppermute | solution.py:322
  73.7 12.9 %collective-permute-start.8 = (bf16[1024,512]{1,0:T(8,128)(2,1)}, bf16[1024,512]{1,0:T(8,128)(2,1)}, u32[]{:S(2)}, u32[]{:S(2)}) collective-permute-start(bf16[1024,512]{1,0:T(8,128)(2,1)} %collective-permute-done.6.refs_1_), channel_id=1, source_target_pairs={{0,8},{8,0},{16,24},{24,16},{1,9},{9,1},{17,25},{25,17},{2,10},{10... | collective-permute-start | bytes 3145736 | tf_op jit(solution)/shard_map/ppermute | solution.py:322
  73.8 8.7 %collective-permute-start.9 = (bf16[512,256]{1,0:T(8,128)(2,1)S(1)}, bf16[512,256]{1,0:T(8,128)(2,1)S(1)}, u32[]{:S(2)}, u32[]{:S(2)}) collective-permute-start(bf16[512,256]{1,0:T(8,128)(2,1)S(1)} %shard_map.74), channel_id=1, source_target_pairs={{0,16},{8,24},{16,0},{24,8},{1,17},{9,25},{17,1},{25,9},{2,18},{10... | collective-permute-start | bytes 786440 | tf_op jit(solution)/shard_map/ppermute | solution.py:322
  82.6 14.8 %collective-permute-start.10 = (bf16[1024,256]{1,0:T(8,128)(2,1)S(1)}, bf16[1024,256]{1,0:T(8,128)(2,1)}, u32[]{:S(2)}, u32[]{:S(2)}) collective-permute-start(bf16[1024,256]{1,0:T(8,128)(2,1)S(1)} %pad_maximum_fusion.1), channel_id=1, source_target_pairs={{0,4},{4,0},{1,5},{5,1},{2,6},{6,2},{3,7},{7,3},{8,12},{12,8},{9,1... | collective-permute-start | bytes 1572872 | tf_op jit(solution)/shard_map/ppermute | solution.py:318
  84.2 24.8 %collective-permute-start.15 = (bf16[1024,512]{1,0:T(8,128)(2,1)}, bf16[1024,512]{1,0:T(8,128)(2,1)}, u32[]{:S(2)}, u32[]{:S(2)}) collective-permute-start(bf16[1024,512]{1,0:T(8,128)(2,1)} %collective-permute-done.14.refs_0_), channel_id=1, source_target_pairs={{0,16},{8,24},{16,0},{24,8},{1,17},{9,25},{17,1},{25,9},{2,18},{10... | collective-permute-start | bytes 3145736 | tf_op jit(solution)/shard_map/ppermute | solution.py:322
  85.2 12.9 %collective-permute-start.11 = (bf16[512,256]{1,0:T(8,128)(2,1)S(1)}, bf16[512,256]{1,0:T(8,128)(2,1)}, u32[]{:S(2)}, u32[]{:S(2)}) collective-permute-start(bf16[512,256]{1,0:T(8,128)(2,1)S(1)} %collective-permute-done.9), channel_id=1, source_target_pairs={{0,8},{8,0},{16,24},{24,16},{1,9},{9,1},{17,25},{25,17},{2,10},{10... | collective-permute-start | bytes 786440 | tf_op jit(solution)/shard_map/ppermute | solution.py:322
  98.0 28.8 %collective-permute-start.16 = (bf16[1024,512]{1,0:T(8,128)(2,1)}, bf16[1024,512]{1,0:T(8,128)(2,1)}, u32[]{:S(2)}, u32[]{:S(2)}) collective-permute-start(bf16[1024,512]{1,0:T(8,128)(2,1)} %collective-permute-done.14.refs_0_), channel_id=1, source_target_pairs={{0,8},{8,0},{16,24},{24,16},{1,9},{9,1},{17,25},{25,17},{2,10},{10... | collective-permute-start | bytes 3145736 | tf_op jit(solution)/shard_map/ppermute | solution.py:322
  109.0 17.8 %collective-permute-start.17 = (bf16[1024,512]{1,0:T(8,128)(2,1)}, bf16[1024,512]{1,0:T(8,128)(2,1)}, u32[]{:S(2)}, u32[]{:S(2)}) collective-permute-start(bf16[1024,512]{1,0:T(8,128)(2,1)} %collective-permute-done.15.refs_1_), channel_id=1, source_target_pairs={{0,8},{8,0},{16,24},{24,16},{1,9},{9,1},{17,25},{25,17},{2,10},{10... | collective-permute-start | bytes 3145736 | tf_op jit(solution)/shard_map/ppermute | solution.py:322
  109.0 14.3 %collective-permute-start.13 = (bf16[512,512]{1,0:T(8,128)(2,1)S(1)}, bf16[512,512]{1,0:T(8,128)(2,1)S(1)}, u32[]{:S(2)}, u32[]{:S(2)}) collective-permute-start(bf16[512,512]{1,0:T(8,128)(2,1)S(1)} %shard_map.76.refs_0_), channel_id=1, source_target_pairs={{0,4},{4,0},{1,5},{5,1},{2,6},{6,2},{3,7},{7,3},{8,12},{12,8},{9,1... | collective-permute-start | bytes 1572872 | tf_op jit(solution)/shard_map/ppermute | solution.py:318
  109.5 61.0 %collective-permute-start.21 = (bf16[256,2048]{1,0:T(8,128)(2,1)S(1)}, bf16[256,2048]{1,0:T(8,128)(2,1)}, u32[]{:S(2)}, u32[]{:S(2)}) collective-permute-start(bf16[256,2048]{1,0:T(8,128)(2,1)S(1)} %dynamic-slice_bitcast_fusion.1.refs_6_), channel_id=1, source_target_pairs={{0,16},{8,24},{16,0},{24,8},{1,17},{9,25},{17,1},{25,9},{2,18},{10... | collective-permute-start | bytes 3145736 | tf_op jit(solution)/shard_map/ppermute | solution.py:322
  124.2 29.5 %collective-permute-start.19 = (bf16[512,512]{1,0:T(8,128)(2,1)}, bf16[512,512]{1,0:T(8,128)(2,1)}, u32[]{:S(2)}, u32[]{:S(2)}) collective-permute-start(bf16[512,512]{1,0:T(8,128)(2,1)} %broadcast_select_fusion), channel_id=1, source_target_pairs={{0,2},{1,3},{2,0},{3,1},{4,6},{5,7},{6,4},{7,5},{8,10},{9,11},{10,... | collective-permute-start | bytes 1572872 | tf_op jit(solution)/shard_map/ppermute | solution.py:322
  158.9 10.8 %collective-permute-start.22 = (bf16[256,512]{1,0:T(8,128)(2,1)S(1)}, bf16[256,512]{1,0:T(8,128)(2,1)S(1)}, u32[]{:S(2)}, u32[]{:S(2)}) collective-permute-start(bf16[256,512]{1,0:T(8,128)(2,1)S(1)} %shard_map.79.refs_1_), channel_id=1, source_target_pairs={{0,4},{4,0},{1,5},{5,1},{2,6},{6,2},{3,7},{7,3},{8,12},{12,8},{9,1... | collective-permute-start | bytes 786440 | tf_op jit(solution)/shard_map/ppermute | solution.py:318
  164.6 24.1 %collective-permute-start.26 = (bf16[256,2048]{1,0:T(8,128)(2,1)S(1)}, bf16[256,2048]{1,0:T(8,128)(2,1)}, u32[]{:S(2)}, u32[]{:S(2)}) collective-permute-start(bf16[256,2048]{1,0:T(8,128)(2,1)S(1)} %dynamic-slice_bitcast_fusion.refs_6_), channel_id=1, source_target_pairs={{0,16},{8,24},{16,0},{24,8},{1,17},{9,25},{17,1},{25,9},{2,18},{10... | collective-permute-start | bytes 3145736 | tf_op jit(solution)/shard_map/ppermute | solution.py:322
  170.6 20.1 %collective-permute-start.23 = (bf16[256,2048]{1,0:T(8,128)(2,1)S(1)}, bf16[256,2048]{1,0:T(8,128)(2,1)}, u32[]{:S(2)}, u32[]{:S(2)}) collective-permute-start(bf16[256,2048]{1,0:T(8,128)(2,1)S(1)} %dynamic-slice_bitcast_fusion.1.refs_6_), channel_id=1, source_target_pairs={{0,8},{8,0},{16,24},{24,16},{1,9},{9,1},{17,25},{25,17},{2,10},{10... | collective-permute-start | bytes 3145736 | tf_op jit(solution)/shard_map/ppermute | solution.py:322
  170.6 20.1 %collective-permute-start.24 = (bf16[256,2048]{1,0:T(8,128)(2,1)}, bf16[256,2048]{1,0:T(8,128)(2,1)}, u32[]{:S(2)}, u32[]{:S(2)}) collective-permute-start(bf16[256,2048]{1,0:T(8,128)(2,1)} %collective-permute-done.21.refs_7_), channel_id=1, source_target_pairs={{0,8},{8,0},{16,24},{24,16},{1,9},{9,1},{17,25},{25,17},{2,10},{10... | collective-permute-start | bytes 3145736 | tf_op jit(solution)/shard_map/ppermute | solution.py:322
  171.1 8.4 %collective-permute-start.18 = (bf16[256,512]{1,0:T(8,128)(2,1)S(1)}, bf16[256,512]{1,0:T(8,128)(2,1)}, u32[]{:S(2)}, u32[]{:S(2)}) collective-permute-start(bf16[256,512]{1,0:T(8,128)(2,1)S(1)} %shard_map.78.refs_1_), channel_id=1, source_target_pairs={{0,4},{4,0},{1,5},{5,1},{2,6},{6,2},{3,7},{7,3},{8,12},{12,8},{9,1... | collective-permute-start | bytes 786440 | tf_op jit(solution)/shard_map/ppermute | solution.py:318
  172.3 17.6 %collective-permute-start.30 = (bf16[256,512]{1,0:T(8,128)(2,1)}, bf16[256,512]{1,0:T(8,128)(2,1)S(1)}, u32[]{:S(2)}, u32[]{:S(2)}) collective-permute-start(bf16[256,512]{1,0:T(8,128)(2,1)} %broadcast_select_fusion.1), channel_id=1, source_target_pairs={{0,2},{1,3},{2,0},{3,1},{4,6},{5,7},{6,4},{7,5},{8,10},{9,11},{10,... | collective-permute-start | bytes 786440 | tf_op jit(solution)/shard_map/ppermute | solution.py:322
  179.5 37.1 %collective-permute-start.27 = (bf16[256,2048]{1,0:T(8,128)(2,1)S(1)}, bf16[256,2048]{1,0:T(8,128)(2,1)S(1)}, u32[]{:S(2)}, u32[]{:S(2)}) collective-permute-start(bf16[256,2048]{1,0:T(8,128)(2,1)S(1)} %dynamic-slice_bitcast_fusion.refs_6_), channel_id=1, source_target_pairs={{0,8},{8,0},{16,24},{24,16},{1,9},{9,1},{17,25},{25,17},{2,10},{10... | collective-permute-start | bytes 3145736 | tf_op jit(solution)/shard_map/ppermute | solution.py:322
  188.7 15.0 %collective-permute-start.20 = (bf16[256,512]{1,0:T(8,128)(2,1)S(1)}, bf16[256,512]{1,0:T(8,128)(2,1)S(1)}, u32[]{:S(2)}, u32[]{:S(2)}) collective-permute-start(bf16[256,512]{1,0:T(8,128)(2,1)S(1)} %broadcast_select_fusion.2), channel_id=1, source_target_pairs={{0,2},{1,3},{2,0},{3,1},{4,6},{5,7},{6,4},{7,5},{8,10},{9,11},{10,... | collective-permute-start | bytes 786440 | tf_op jit(solution)/shard_map/ppermute | solution.py:322
  189.8 26.7 %collective-permute-start.28 = (bf16[256,2048]{1,0:T(8,128)(2,1)}, bf16[256,2048]{1,0:T(8,128)(2,1)S(1)}, u32[]{:S(2)}, u32[]{:S(2)}) collective-permute-start(bf16[256,2048]{1,0:T(8,128)(2,1)} %collective-permute-done.26.refs_7_), channel_id=1, source_target_pairs={{0,8},{8,0},{16,24},{24,16},{1,9},{9,1},{17,25},{25,17},{2,10},{10... | collective-permute-start | bytes 3145736 | tf_op jit(solution)/shard_map/ppermute | solution.py:322
  201.6 14.8 %collective-permute-start.31 = (bf16[128,2048]{1,0:T(8,128)(2,1)S(1)}, bf16[128,2048]{1,0:T(8,128)(2,1)S(1)}, u32[]{:S(2)}, u32[]{:S(2)}) collective-permute-start(bf16[128,2048]{1,0:T(8,128)(2,1)S(1)} %get-tuple-element.66), channel_id=1, source_target_pairs={{0,1},{1,0},{2,3},{3,2},{4,5},{5,4},{6,7},{7,6},{8,9},{9,8},{10,11... | collective-permute-start | bytes 1572872 | tf_op jit(solution)/shard_map/ppermute | solution.py:322
  209.6 19.1 %collective-permute-start.25 = (bf16[128,2048]{1,0:T(8,128)(2,1)S(1)}, bf16[128,2048]{1,0:T(8,128)(2,1)S(1)}, u32[]{:S(2)}, u32[]{:S(2)}) collective-permute-start(bf16[128,2048]{1,0:T(8,128)(2,1)S(1)} %get-tuple-element.59), channel_id=1, source_target_pairs={{0,1},{1,0},{2,3},{3,2},{4,5},{5,4},{6,7},{7,6},{8,9},{9,8},{10,11... | collective-permute-start | bytes 1572872 | tf_op jit(solution)/shard_map/ppermute | solution.py:322
  221.6 17.3 %collective-permute-start.32 = (bf16[128,2048]{1,0:T(8,128)(2,1)S(1)}, bf16[128,2048]{1,0:T(8,128)(2,1)S(1)}, u32[]{:S(2)}, u32[]{:S(2)}) collective-permute-start(bf16[128,2048]{1,0:T(8,128)(2,1)S(1)} %get-tuple-element.68), channel_id=1, source_target_pairs={{0,1},{1,0},{2,3},{3,2},{4,5},{5,4},{6,7},{7,6},{8,9},{9,8},{10,11... | collective-permute-start | bytes 1572872 | tf_op jit(solution)/shard_map/ppermute | solution.py:322
  228.0 21.2 %collective-permute-start.29 = (bf16[128,2048]{1,0:T(8,128)(2,1)S(1)}, bf16[128,2048]{1,0:T(8,128)(2,1)S(1)}, u32[]{:S(2)}, u32[]{:S(2)}) collective-permute-start(bf16[128,2048]{1,0:T(8,128)(2,1)S(1)} %get-tuple-element.64), channel_id=1, source_target_pairs={{0,1},{1,0},{2,3},{3,2},{4,5},{5,4},{6,7},{7,6},{8,9},{9,8},{10,11... | collective-permute-start | bytes 1572872 | tf_op jit(solution)/shard_map/ppermute | solution.py:322
  (23 other events, 130.2 us)
Sparse Core Ops, SparseCore 0:
  13.9 56.8 all-gather.4
  73.8 71.9 all-gather.6

commit v2 on v1

--- a/solution.py
+++ b/solution.py
@@ -408,7 +408,7 @@
     b_y = after(b_y, pair_x)
     b_yx = along(b_y)
     queries_a = project(
-        "queries_a", own, after(rest, w0_z), pieces, weights, 0, 4, tables
+        "queries_a", own, after(rest, b_y, w0_z), pieces, weights, 0, 4, tables
     )
     two_y = after(two_y, queries_a)
     pairs = (
@@ -442,7 +442,7 @@
     w1_z = after(w1_z, att_b[0])
     w1_zx = along(w1_z)
 
-    late = sent
+    late = queries_b
     w_quarters = [
         [w0_z, w0_zx, across(after(w0_z, late)), across(after(w0_zx, late))],
         [w1_z, w1_zx, across(after(w1_z, late)), across(after(w1_zx, late))],

time: 263 us -> 266 us (1.011)
  Pallas kernels: 68.6 us -> 87.9 us
  starting transfers between devices: 36.8 us -> 26.7 us
  waiting for transfers between devices: 99.2 us -> 95.7 us
    pallas_call x11, Pallas kernels: 68.6 us -> 87.9 us  [call(): pl.pallas_call(kernel, in_specs=specs, out_specs=[VMEM] * len(shapes), ou...]
    all_gather x2, waiting for transfers between devices: 8.1 us -> 0.01 us  [two_along_tp(): lax.all_gather(piece, 'tp', axis=0, axis_index_groups=[[0, 2], [1, 3]])]
    ppermute x7, starting transfers between devices: 13.5 us -> 8.25 us  [swap_uly(): return lax.ppermute(array, 'uly', [(0, 1), (1, 0)])]
    ppermute x26, starting transfers between devices: 23.2 us -> 18.4 us  [swap(): return lax.ppermute(array, name, [(i, i ^ bit) for i in range(4)])]
    ppermute x7, waiting for transfers between devices: 22.5 us -> 25.4 us  [swap_uly(): return lax.ppermute(array, 'uly', [(0, 1), (1, 0)])]
    unnamed x42 -> x30, local copies, waits for them, and re-layouts: 17.1 us -> 15.2 us
  transfers between devices with their start and end apart: 35 -> 35, of which waited for: 17 -> 13; matrix products, arithmetic and copies ran while one was open for 7% -> 7% of each run, Pallas kernels for 27% -> 34%
where the time goes in v2:
time: 266 us; the launch traced here: 262 us
  waiting for transfers between devices  95.7 us (36%)
  Pallas kernels  87.9 us (33%)
  starting transfers between devices  26.7 us (10%)
  local copies, waits for them, and re-layouts  25.7 us (10%)
  between operations  17.2 us (6%)
  other arithmetic  9.01 us (3%)
    pallas_call x11, Pallas kernels, call(): pl.pallas_call(kernel, in_specs=specs, out_specs=[VMEM] * len(shapes), ou...  87.9 us
    ppermute x26, waiting for transfers between devices, swap(): return lax.ppermute(array, name, [(i, i ^ bit) for i in range(4)])  70.2 us
    ppermute x7, waiting for transfers between devices, swap_uly(): return lax.ppermute(array, 'uly', [(0, 1), (1, 0)])  25.4 us
    ppermute x26, starting transfers between devices, swap(): return lax.ppermute(array, name, [(i, i ^ bit) for i in range(4)])  18.4 us
    unnamed x30, local copies, waits for them, and re-layouts  15.2 us
    ppermute x7, starting transfers between devices, swap_uly(): return lax.ppermute(array, 'uly', [(0, 1), (1, 0)])  8.25 us
  transfers between devices with their start and end apart: 35, of which 13 were waited for; matrix products, arithmetic and copies ran while one was open for 7% of the time, Pallas kernels for 34%

profile of v2, /device:TPU:0, one launch (start us, length us, event | category | flops | bytes accessed | tf_op | source)
XLA Modules:
  0.0 262.2 jit_solution(14076982823397635672)
XLA Ops:
  7.6 3.0 %collective-permute-start = (bf16[1024,256]{1,0:T(8,128)(2,1)S(1)}, bf16[1024,256]{1,0:T(8,128)(2,1)S(1)}, u32[]{:S(2)}, u32[]{:S(2)}) collective-permute-start(bf16[1024,256]{1,0:T(8,128)(2,1)S(1)} %dynamic-slice_bitcast_fusion.4), channel_id=1, source_target_pairs={{0,4},{4,0},{1,5},{5,1},{2,6},{6,2},{3,7},{7,3},{8,12},{12,8},{9,1... | collective-permute-start | bytes 1572872 | tf_op jit(solution)/shard_map/ppermute | solution.py:318
  10.7 3.1 %constant_dynamic-slice_fusion.1 = (bf16[256,2048]{1,0:T(8,128)(2,1)}, bf16[256,2048]{1,0:T(8,128)(2,1)}) fusion(bf16[1024,4096]{1,0:T(8,128)(2,1)} %refs_10_.7, s32[]{:T(128)S(6)} %select_n.82), kind=kLoop, calls=%fused_computation.40 | loop fusion | bytes 4194308 | tf_op jit(solution)/shard_map/dynamic_slice | solution.py:345
  13.8 3.0 %dynamic-slice_bitcast_fusion.2 = (bf16[1024,512]{1,0:T(8,128)(2,1)}, bf16[1024,512]{1,0:T(8,128)(2,1)}) fusion(bf16[4096,1,1280]{2,0,1:T(8,128)(2,1)} %param.9, s32[]{:T(128)S(6)} %select_n.81), kind=kLoop, calls=%fused_computation.9 | loop fusion | bytes 4194308 | tf_op jit(solution)/shard_map/dynamic_slice | solution.py:342
  19.4 4.0 %collective-permute-done.refs_0_ = bf16[1024,256]{1,0:T(8,128)(2,1)S(1)} collective-permute-done((bf16[1024,256]{1,0:T(8,128)(2,1)S(1)}, bf16[1024,256]{1,0:T(8,128)(2,1)S(1)}, u32[]{:S(2)}, u32[]{:S(2)}) %collective-permute-start) | collective-permute-done | bytes 524320 | tf_op jit(solution)/shard_map/ppermute | solution.py:318
  23.4 2.0 collective-permute-start.1
  25.6 10.0 %shard_map.73 = (bf16[512,4096]{1,0:T(8,128)(2,1)}, bf16[512,4096]{1,0:T(8,128)(2,1)}) custom-call(s32[5]{0:T(128)S(1)} %pad_add_fusion.1.start_ref, bf16[512,8192]{1,0:T(8,128)(2,1)} %hidden_ref, bf16[1,8192]{1,0:T(2,128)(2,1)S(1)} %reshape.41.gain_ref), custom_call_target="tpu_custom_call" | custom-call | flops 4000000000 | tf_op jit(solution)/shard_map/pallas_call | solution.py:51
  37.7 2.2 copy-done.1
  39.9 6.4 %shard_map.74 = bf16[512,256]{1,0:T(8,128)(2,1)S(1)} custom-call(bf16[512,4096]{1,0:T(8,128)(2,1)S(1)} %copy-done.1, bf16[512,4096]{1,0:T(8,128)(2,1)} %get-tuple-element.51.rest_ref, bf16[1024,256]{1,0:T(8,128)(2,1)S(1)} %collective-permute-done.refs_0_, bf16[1024,256]{1,0:T(8,128)(2,1)S(1)} %collective-permute-done.1.refs_1_, ...), custom_call_target="tpu_custom_call" | custom-call | flops 1000000000 | tf_op jit(solution)/shard_map/pallas_call | solution.py:51
  50.7 22.9 %collective-permute-done.8.refs_1_ = bf16[1024,512]{1,0:T(8,128)(2,1)} collective-permute-done((bf16[1024,512]{1,0:T(8,128)(2,1)}, bf16[1024,512]{1,0:T(8,128)(2,1)}, u32[]{:S(2)}, u32[]{:S(2)}) %collective-permute-start.8) | collective-permute-done | bytes 1048608 | tf_op jit(solution)/shard_map/ppermute | solution.py:322
  79.7 2.8 %collective-permute-done.5 = bf16[512,256]{1,0:T(8,128)(2,1)S(1)} collective-permute-done((bf16[512,256]{1,0:T(8,128)(2,1)S(1)}, bf16[512,256]{1,0:T(8,128)(2,1)S(1)}, u32[]{:S(2)}, u32[]{:S(2)}) %collective-permute-start.5) | collective-permute-done | bytes 262176 | tf_op jit(solution)/shard_map/ppermute | solution.py:322
  86.6 2.2 copy-done.2
  88.8 8.7 %shard_map.75.q_ref = bf16[512,512]{1,0:T(8,128)(2,1)S(1)} custom-call(bf16[512,4096]{1,0:T(8,128)(2,1)S(1)} %copy-done.2, bf16[512,4096]{1,0:T(8,128)(2,1)} %get-tuple-element.51.rest_ref, bf16[1024,512]{1,0:T(8,128)(2,1)} %collective-permute-done.6.refs_0_, bf16[1024,512]{1,0:T(8,128)(2,1)} %collective-permute-done.8.refs_1_, ...), custom_call_target="tpu_custom_call" | custom-call | flops 4000000000 | tf_op jit(solution)/shard_map/pallas_call | solution.py:51
  100.3 12.5 %shard_map.76.refs_0_ = bf16[512,512]{1,0:T(8,128)(2,1)S(1)} custom-call(s32[10]{0:T(128)S(1)} %pad_add_fusion.2.info_ref, bf16[512,512]{1,0:T(8,128)(2,1)S(1)} %shard_map.75.q_ref, s32[1,512]{1,0:T(1,128)S(1)} %bitcast.28, bf16[2048,256]{1,0:T(8,128)(2,1)S(1)} %pad_maximum_fusion.refs_0_, bf16[2048,256]{1,0:T(8,128)(2,1)S(1)} %constant_dynamic-update-slice_fusion.refs_1_), custom_call_target="tpu_custom_call" | custom-call | flops 4000000000 | tf_op jit(solution)/shard_map/pallas_call | solution.py:51
  113.1 14.2 %collective-permute-done.14.refs_2_ = bf16[512,512]{1,0:T(8,128)(2,1)S(1)} collective-permute-done((bf16[512,512]{1,0:T(8,128)(2,1)S(1)}, bf16[512,512]{1,0:T(8,128)(2,1)S(1)}, u32[]{:S(2)}, u32[]{:S(2)}) %collective-permute-start.14) | collective-permute-done | bytes 524320 | tf_op jit(solution)/shard_map/ppermute | solution.py:318
  128.1 2.6 collective-permute-start.19
  130.7 2.2 copy-done.3
  132.9 8.7 %shard_map.77.q_ref = bf16[512,512]{1,0:T(8,128)(2,1)S(1)} custom-call(bf16[512,4096]{1,0:T(8,128)(2,1)S(1)} %copy-done.3, bf16[512,4096]{1,0:T(8,128)(2,1)} %get-tuple-element.51.rest_ref, bf16[1024,512]{1,0:T(8,128)(2,1)} %collective-permute-done.4.refs_0_, bf16[1024,512]{1,0:T(8,128)(2,1)} %collective-permute-done.15.refs_1_, ...), custom_call_target="tpu_custom_call" | custom-call | flops 1000000 | tf_op jit(solution)/shard_map/pallas_call | solution.py:51
  147.2 9.5 %shard_map.78.refs_1_ = bf16[256,512]{1,0:T(8,128)(2,1)S(1)} custom-call(s32[10]{0:T(128)S(1)} %pad_add_fusion.2.info_ref, bf16[512,512]{1,0:T(8,128)(2,1)S(1)} %copy-done.7, s32[1,512]{1,0:T(1,128)S(1)} %bitcast.29, bf16[2048,256]{1,0:T(8,128)(2,1)S(1)} %copy-done.5, bf16[2048,256]{1,0:T(8,128)(2,1)S(1)} %copy-done.9), custom_call_target="tpu_custom_call" | custom-call | flops 4000000000 | tf_op jit(solution)/shard_map/pallas_call | solution.py:51
  156.8 2.3 collective-permute-start.25
  159.6 10.4 %shard_map.81.refs_1_ = bf16[256,512]{1,0:T(8,128)(2,1)} custom-call(s32[10]{0:T(128)S(1)} %pad_add_fusion.2.info_ref, bf16[512,512]{1,0:T(8,128)(2,1)S(1)} %copy-done.7, s32[1,512]{1,0:T(1,128)S(1)} %bitcast.30, bf16[2048,256]{1,0:T(8,128)(2,1)S(1)} %copy-done.5, bf16[2048,256]{1,0:T(8,128)(2,1)S(1)} %copy-done.9), custom_call_target="tpu_custom_call" | custom-call | flops 4000000000 | tf_op jit(solution)/shard_map/pallas_call | solution.py:51
  169.9 2.0 collective-permute-start.18
  171.9 5.7 %collective-permute-done.29.refs_3_ = bf16[256,512]{1,0:T(8,128)(2,1)} collective-permute-done((bf16[256,512]{1,0:T(8,128)(2,1)}, bf16[256,512]{1,0:T(8,128)(2,1)}, u32[]{:S(2)}, u32[]{:S(2)}) %collective-permute-start.29) | collective-permute-done | bytes 262176 | tf_op jit(solution)/shard_map/ppermute | solution.py:318
  181.8 14.2 %collective-permute-done.30.refs_5_ = bf16[256,512]{1,0:T(8,128)(2,1)S(1)} collective-permute-done((bf16[256,512]{1,0:T(8,128)(2,1)S(1)}, bf16[256,512]{1,0:T(8,128)(2,1)S(1)}, u32[]{:S(2)}, u32[]{:S(2)}) %collective-permute-start.30) | collective-permute-done | bytes 262176 | tf_op jit(solution)/shard_map/ppermute | solution.py:322
  196.0 3.4 %copy-done = bf16[1024,4096]{1,0:T(8,128)(2,1)S(1)} copy-done((bf16[1024,4096]{1,0:T(8,128)(2,1)S(1)}, bf16[1024,4096]{1,0:T(8,128)(2,1)}, u32[]{:S(2)}) %copy-start) | copy-done | bytes 8388632
  199.4 5.8 %shard_map.82 = (f32[128,2048]{1,0:T(8,128)S(1)}, bf16[128,2048]{1,0:T(8,128)(2,1)S(1)}) custom-call(s32[6]{0:T(128)S(1)} %pad_add_fusion.info_ref, bf16[512,512]{1,0:T(8,128)(2,1)S(1)} %shard_map.76.refs_0_, bf16[256,512]{1,0:T(8,128)(2,1)} %shard_map.81.refs_1_, bf16[512,512]{1,0:T(8,128)(2,1)S(1)} %collective-permute-done.14.refs_2_, ...), custom_call_target="tpu_custom_call" | custom-call | flops 4000000000 | tf_op jit(solution)/shard_map/pallas_call | solution.py:51
  205.3 5.9 %shard_map.79 = (f32[128,2048]{1,0:T(8,128)S(1)}, bf16[128,2048]{1,0:T(8,128)(2,1)S(1)}) custom-call(s32[6]{0:T(128)S(1)} %pad_add_fusion.info_ref, bf16[512,512]{1,0:T(8,128)(2,1)S(1)} %shard_map.76.refs_0_, bf16[256,512]{1,0:T(8,128)(2,1)S(1)} %shard_map.78.refs_1_, bf16[512,512]{1,0:T(8,128)(2,1)S(1)} %collective-permute-done.14.refs_2_, ...), custom_call_target="tpu_custom_call" | custom-call | flops 4000000000 | tf_op jit(solution)/shard_map/pallas_call | solution.py:51
  211.1 2.1 collective-permute-start.24
  213.2 6.8 %collective-permute-done.31 = bf16[128,2048]{1,0:T(8,128)(2,1)S(1)} collective-permute-done((bf16[128,2048]{1,0:T(8,128)(2,1)S(1)}, bf16[128,2048]{1,0:T(8,128)(2,1)S(1)}, u32[]{:S(2)}, u32[]{:S(2)}) %collective-permute-start.31) | collective-permute-done | bytes 524320 | tf_op jit(solution)/shard_map/ppermute | solution.py:322
  220.1 5.1 %shard_map.83 = (f32[128,2048]{1,0:T(8,128)S(1)}, bf16[128,2048]{1,0:T(8,128)(2,1)S(1)}) custom-call(s32[6]{0:T(128)S(1)} %pad_add_fusion.info_ref, bf16[512,512]{1,0:T(8,128)(2,1)S(1)} %shard_map.76.refs_0_, bf16[256,512]{1,0:T(8,128)(2,1)} %shard_map.81.refs_1_, bf16[512,512]{1,0:T(8,128)(2,1)S(1)} %collective-permute-done.14.refs_2_, ...), custom_call_target="tpu_custom_call" | custom-call | flops 4000000000 | tf_op jit(solution)/shard_map/pallas_call | solution.py:51
  225.4 5.0 %shard_map.80 = (f32[128,2048]{1,0:T(8,128)S(1)}, bf16[128,2048]{1,0:T(8,128)(2,1)S(1)}) custom-call(s32[6]{0:T(128)S(1)} %pad_add_fusion.info_ref, bf16[512,512]{1,0:T(8,128)(2,1)S(1)} %shard_map.76.refs_0_, bf16[256,512]{1,0:T(8,128)(2,1)S(1)} %shard_map.78.refs_1_, bf16[512,512]{1,0:T(8,128)(2,1)S(1)} %collective-permute-done.14.refs_2_, ...), custom_call_target="tpu_custom_call" | custom-call | flops 4000000000 | tf_op jit(solution)/shard_map/pallas_call | solution.py:51
  232.5 9.9 %collective-permute-done.32 = bf16[128,2048]{1,0:T(8,128)(2,1)S(1)} collective-permute-done((bf16[128,2048]{1,0:T(8,128)(2,1)S(1)}, bf16[128,2048]{1,0:T(8,128)(2,1)S(1)}, u32[]{:S(2)}, u32[]{:S(2)}) %collective-permute-start.32) | collective-permute-done | bytes 524320 | tf_op jit(solution)/shard_map/ppermute | solution.py:322
  242.6 10.7 %collective-permute-done.28 = bf16[128,2048]{1,0:T(8,128)(2,1)S(1)} collective-permute-done((bf16[128,2048]{1,0:T(8,128)(2,1)S(1)}, bf16[128,2048]{1,0:T(8,128)(2,1)S(1)}, u32[]{:S(2)}, u32[]{:S(2)}) %collective-permute-start.28) | collective-permute-done | bytes 524320 | tf_op jit(solution)/shard_map/ppermute | solution.py:322
  (113 shorter events, 35.8 us)
Async XLA Ops:
  6.5 78.7 %all-gather.5.cloned.1.call-start = ((), (), s32[]{:S(2)}) async-start(), calls=%async_computation | async-start | bytes 3145728 | tf_op jit(solution)/shard_map/all_gather | solution.py:359
  7.6 15.8 %collective-permute-start = (bf16[1024,256]{1,0:T(8,128)(2,1)S(1)}, bf16[1024,256]{1,0:T(8,128)(2,1)S(1)}, u32[]{:S(2)}, u32[]{:S(2)}) collective-permute-start(bf16[1024,256]{1,0:T(8,128)(2,1)S(1)} %dynamic-slice_bitcast_fusion.4), channel_id=1, source_target_pairs={{0,4},{4,0},{1,5},{5,1},{2,6},{6,2},{3,7},{7,3},{8,12},{12,8},{9,1... | collective-permute-start | bytes 1572872 | tf_op jit(solution)/shard_map/ppermute | solution.py:318
  13.8 128.6 %all-gather.7.cloned.1.call-start = ((), (), s32[]{:S(2)}) async-start(), calls=%async_computation.1 | async-start | bytes 3145728 | tf_op jit(solution)/shard_map/all_gather | solution.py:359
  16.8 29.9 %collective-permute-start.6 = (bf16[1024,512]{1,0:T(8,128)(2,1)}, bf16[1024,512]{1,0:T(8,128)(2,1)}, u32[]{:S(2)}, u32[]{:S(2)}) collective-permute-start(bf16[1024,512]{1,0:T(8,128)(2,1)} %get-tuple-element.70), channel_id=1, source_target_pairs={{0,4},{4,0},{1,5},{5,1},{2,6},{6,2},{3,7},{7,3},{8,12},{12,8},{9,1... | collective-permute-start | bytes 3145736 | tf_op jit(solution)/shard_map/ppermute | solution.py:318
  23.4 12.3 %collective-permute-start.1 = (bf16[1024,256]{1,0:T(8,128)(2,1)S(1)}, bf16[1024,256]{1,0:T(8,128)(2,1)S(1)}, u32[]{:S(2)}, u32[]{:S(2)}) collective-permute-start(bf16[1024,256]{1,0:T(8,128)(2,1)S(1)} %collective-permute-done.refs_0_), channel_id=1, source_target_pairs={{0,16},{8,24},{16,0},{24,8},{1,17},{9,25},{17,1},{25,9},{2,18},{10... | collective-permute-start | bytes 1572872 | tf_op jit(solution)/shard_map/ppermute | solution.py:322
  25.5 10.6 %collective-permute-start.2 = (bf16[1024,256]{1,0:T(8,128)(2,1)S(1)}, bf16[1024,256]{1,0:T(8,128)(2,1)S(1)}, u32[]{:S(2)}, u32[]{:S(2)}) collective-permute-start(bf16[1024,256]{1,0:T(8,128)(2,1)S(1)} %collective-permute-done.refs_0_), channel_id=1, source_target_pairs={{0,8},{8,0},{16,24},{24,16},{1,9},{9,1},{17,25},{25,17},{2,10},{10... | collective-permute-start | bytes 1572872 | tf_op jit(solution)/shard_map/ppermute | solution.py:322
  47.9 25.8 %collective-permute-start.8 = (bf16[1024,512]{1,0:T(8,128)(2,1)}, bf16[1024,512]{1,0:T(8,128)(2,1)}, u32[]{:S(2)}, u32[]{:S(2)}) collective-permute-start(bf16[1024,512]{1,0:T(8,128)(2,1)} %collective-permute-done.6.refs_0_), channel_id=1, source_target_pairs={{0,16},{8,24},{16,0},{24,8},{1,17},{9,25},{17,1},{25,9},{2,18},{10... | collective-permute-start | bytes 3145736 | tf_op jit(solution)/shard_map/ppermute | solution.py:322
  49.2 30.5 %collective-permute-start.4 = (bf16[1024,512]{1,0:T(8,128)(2,1)}, bf16[1024,512]{1,0:T(8,128)(2,1)}, u32[]{:S(2)}, u32[]{:S(2)}) collective-permute-start(bf16[1024,512]{1,0:T(8,128)(2,1)} %get-tuple-element.69), channel_id=1, source_target_pairs={{0,4},{4,0},{1,5},{5,1},{2,6},{6,2},{3,7},{7,3},{8,12},{12,8},{9,1... | collective-permute-start | bytes 3145736 | tf_op jit(solution)/shard_map/ppermute | solution.py:318
  50.7 35.8 %collective-permute-start.9 = (bf16[1024,512]{1,0:T(8,128)(2,1)}, bf16[1024,512]{1,0:T(8,128)(2,1)}, u32[]{:S(2)}, u32[]{:S(2)}) collective-permute-start(bf16[1024,512]{1,0:T(8,128)(2,1)} %collective-permute-done.6.refs_0_), channel_id=1, source_target_pairs={{0,8},{8,0},{16,24},{24,16},{1,9},{9,1},{17,25},{25,17},{2,10},{10... | collective-permute-start | bytes 3145736 | tf_op jit(solution)/shard_map/ppermute | solution.py:322
  73.7 12.9 %collective-permute-start.10 = (bf16[1024,512]{1,0:T(8,128)(2,1)}, bf16[1024,512]{1,0:T(8,128)(2,1)}, u32[]{:S(2)}, u32[]{:S(2)}) collective-permute-start(bf16[1024,512]{1,0:T(8,128)(2,1)} %collective-permute-done.8.refs_1_), channel_id=1, source_target_pairs={{0,8},{8,0},{16,24},{24,16},{1,9},{9,1},{17,25},{25,17},{2,10},{10... | collective-permute-start | bytes 3145736 | tf_op jit(solution)/shard_map/ppermute | solution.py:322
  73.8 8.7 %collective-permute-start.5 = (bf16[512,256]{1,0:T(8,128)(2,1)S(1)}, bf16[512,256]{1,0:T(8,128)(2,1)S(1)}, u32[]{:S(2)}, u32[]{:S(2)}) collective-permute-start(bf16[512,256]{1,0:T(8,128)(2,1)S(1)} %shard_map.74), channel_id=1, source_target_pairs={{0,16},{8,24},{16,0},{24,8},{1,17},{9,25},{17,1},{25,9},{2,18},{10... | collective-permute-start | bytes 786440 | tf_op jit(solution)/shard_map/ppermute | solution.py:322
  82.6 14.8 %collective-permute-start.11 = (bf16[1024,256]{1,0:T(8,128)(2,1)S(1)}, bf16[1024,256]{1,0:T(8,128)(2,1)}, u32[]{:S(2)}, u32[]{:S(2)}) collective-permute-start(bf16[1024,256]{1,0:T(8,128)(2,1)S(1)} %pad_maximum_fusion.1), channel_id=1, source_target_pairs={{0,4},{4,0},{1,5},{5,1},{2,6},{6,2},{3,7},{7,3},{8,12},{12,8},{9,1... | collective-permute-start | bytes 1572872 | tf_op jit(solution)/shard_map/ppermute | solution.py:318
  84.2 28.6 %collective-permute-start.15 = (bf16[1024,512]{1,0:T(8,128)(2,1)}, bf16[1024,512]{1,0:T(8,128)(2,1)}, u32[]{:S(2)}, u32[]{:S(2)}) collective-permute-start(bf16[1024,512]{1,0:T(8,128)(2,1)} %collective-permute-done.4.refs_0_), channel_id=1, source_target_pairs={{0,16},{8,24},{16,0},{24,8},{1,17},{9,25},{17,1},{25,9},{2,18},{10... | collective-permute-start | bytes 3145736 | tf_op jit(solution)/shard_map/ppermute | solution.py:322
  85.2 12.9 %collective-permute-start.12 = (bf16[512,256]{1,0:T(8,128)(2,1)S(1)}, bf16[512,256]{1,0:T(8,128)(2,1)}, u32[]{:S(2)}, u32[]{:S(2)}) collective-permute-start(bf16[512,256]{1,0:T(8,128)(2,1)S(1)} %collective-permute-done.5), channel_id=1, source_target_pairs={{0,8},{8,0},{16,24},{24,16},{1,9},{9,1},{17,25},{25,17},{2,10},{10... | collective-permute-start | bytes 786440 | tf_op jit(solution)/shard_map/ppermute | solution.py:322
  98.0 32.7 %collective-permute-start.16 = (bf16[1024,512]{1,0:T(8,128)(2,1)}, bf16[1024,512]{1,0:T(8,128)(2,1)}, u32[]{:S(2)}, u32[]{:S(2)}) collective-permute-start(bf16[1024,512]{1,0:T(8,128)(2,1)} %collective-permute-done.4.refs_0_), channel_id=1, source_target_pairs={{0,8},{8,0},{16,24},{24,16},{1,9},{9,1},{17,25},{25,17},{2,10},{10... | collective-permute-start | bytes 3145736 | tf_op jit(solution)/shard_map/ppermute | solution.py:322
  112.8 17.9 %collective-permute-start.17 = (bf16[1024,512]{1,0:T(8,128)(2,1)}, bf16[1024,512]{1,0:T(8,128)(2,1)}, u32[]{:S(2)}, u32[]{:S(2)}) collective-permute-start(bf16[1024,512]{1,0:T(8,128)(2,1)} %collective-permute-done.15.refs_1_), channel_id=1, source_target_pairs={{0,8},{8,0},{16,24},{24,16},{1,9},{9,1},{17,25},{25,17},{2,10},{10... | collective-permute-start | bytes 3145736 | tf_op jit(solution)/shard_map/ppermute | solution.py:322
  112.9 14.3 %collective-permute-start.14 = (bf16[512,512]{1,0:T(8,128)(2,1)S(1)}, bf16[512,512]{1,0:T(8,128)(2,1)S(1)}, u32[]{:S(2)}, u32[]{:S(2)}) collective-permute-start(bf16[512,512]{1,0:T(8,128)(2,1)S(1)} %shard_map.76.refs_0_), channel_id=1, source_target_pairs={{0,4},{4,0},{1,5},{5,1},{2,6},{6,2},{3,7},{7,3},{8,12},{12,8},{9,1... | collective-permute-start | bytes 1572872 | tf_op jit(solution)/shard_map/ppermute | solution.py:318
  113.0 46.1 %collective-permute-start.21 = (bf16[256,2048]{1,0:T(8,128)(2,1)S(1)}, bf16[256,2048]{1,0:T(8,128)(2,1)}, u32[]{:S(2)}, u32[]{:S(2)}) collective-permute-start(bf16[256,2048]{1,0:T(8,128)(2,1)S(1)} %dynamic-slice_bitcast_fusion.1.refs_6_), channel_id=1, source_target_pairs={{0,16},{8,24},{16,0},{24,8},{1,17},{9,25},{17,1},{25,9},{2,18},{10... | collective-permute-start | bytes 3145736 | tf_op jit(solution)/shard_map/ppermute | solution.py:322
  128.1 28.6 %collective-permute-start.19 = (bf16[512,512]{1,0:T(8,128)(2,1)}, bf16[512,512]{1,0:T(8,128)(2,1)}, u32[]{:S(2)}, u32[]{:S(2)}) collective-permute-start(bf16[512,512]{1,0:T(8,128)(2,1)} %broadcast_select_fusion), channel_id=1, source_target_pairs={{0,2},{1,3},{2,0},{3,1},{4,6},{5,7},{6,4},{7,5},{8,10},{9,11},{10,... | collective-permute-start | bytes 1572872 | tf_op jit(solution)/shard_map/ppermute | solution.py:322
  156.8 23.6 %collective-permute-start.25 = (bf16[256,2048]{1,0:T(8,128)(2,1)S(1)}, bf16[256,2048]{1,0:T(8,128)(2,1)}, u32[]{:S(2)}, u32[]{:S(2)}) collective-permute-start(bf16[256,2048]{1,0:T(8,128)(2,1)S(1)} %dynamic-slice_bitcast_fusion.refs_6_), channel_id=1, source_target_pairs={{0,16},{8,24},{16,0},{24,8},{1,17},{9,25},{17,1},{25,9},{2,18},{10... | collective-permute-start | bytes 3145736 | tf_op jit(solution)/shard_map/ppermute | solution.py:322
  159.0 37.0 %collective-permute-start.22 = (bf16[256,2048]{1,0:T(8,128)(2,1)S(1)}, bf16[256,2048]{1,0:T(8,128)(2,1)}, u32[]{:S(2)}, u32[]{:S(2)}) collective-permute-start(bf16[256,2048]{1,0:T(8,128)(2,1)S(1)} %dynamic-slice_bitcast_fusion.1.refs_6_), channel_id=1, source_target_pairs={{0,8},{8,0},{16,24},{24,16},{1,9},{9,1},{17,25},{25,17},{2,10},{10... | collective-permute-start | bytes 3145736 | tf_op jit(solution)/shard_map/ppermute | solution.py:322
  159.1 37.0 %collective-permute-start.23 = (bf16[256,2048]{1,0:T(8,128)(2,1)}, bf16[256,2048]{1,0:T(8,128)(2,1)}, u32[]{:S(2)}, u32[]{:S(2)}) collective-permute-start(bf16[256,2048]{1,0:T(8,128)(2,1)} %collective-permute-done.21.refs_7_), channel_id=1, source_target_pairs={{0,8},{8,0},{16,24},{24,16},{1,9},{9,1},{17,25},{25,17},{2,10},{10... | collective-permute-start | bytes 3145736 | tf_op jit(solution)/shard_map/ppermute | solution.py:322
  169.9 7.7 %collective-permute-start.29 = (bf16[256,512]{1,0:T(8,128)(2,1)}, bf16[256,512]{1,0:T(8,128)(2,1)}, u32[]{:S(2)}, u32[]{:S(2)}) collective-permute-start(bf16[256,512]{1,0:T(8,128)(2,1)} %shard_map.81.refs_1_), channel_id=1, source_target_pairs={{0,4},{4,0},{1,5},{5,1},{2,6},{6,2},{3,7},{7,3},{8,12},{12,8},{9,1... | collective-permute-start | bytes 786440 | tf_op jit(solution)/shard_map/ppermute | solution.py:318
  169.9 10.4 %collective-permute-start.18 = (bf16[256,512]{1,0:T(8,128)(2,1)S(1)}, bf16[256,512]{1,0:T(8,128)(2,1)S(1)}, u32[]{:S(2)}, u32[]{:S(2)}) collective-permute-start(bf16[256,512]{1,0:T(8,128)(2,1)S(1)} %shard_map.78.refs_1_), channel_id=1, source_target_pairs={{0,4},{4,0},{1,5},{5,1},{2,6},{6,2},{3,7},{7,3},{8,12},{12,8},{9,1... | collective-permute-start | bytes 786440 | tf_op jit(solution)/shard_map/ppermute | solution.py:318
  178.6 17.4 %collective-permute-start.30 = (bf16[256,512]{1,0:T(8,128)(2,1)S(1)}, bf16[256,512]{1,0:T(8,128)(2,1)S(1)}, u32[]{:S(2)}, u32[]{:S(2)}) collective-permute-start(bf16[256,512]{1,0:T(8,128)(2,1)S(1)} %broadcast_select_fusion.1), channel_id=1, source_target_pairs={{0,2},{1,3},{2,0},{3,1},{4,6},{5,7},{6,4},{7,5},{8,10},{9,11},{10,... | collective-permute-start | bytes 786440 | tf_op jit(solution)/shard_map/ppermute | solution.py:322
  180.3 39.8 %collective-permute-start.26 = (bf16[256,2048]{1,0:T(8,128)(2,1)S(1)}, bf16[256,2048]{1,0:T(8,128)(2,1)S(1)}, u32[]{:S(2)}, u32[]{:S(2)}) collective-permute-start(bf16[256,2048]{1,0:T(8,128)(2,1)S(1)} %dynamic-slice_bitcast_fusion.refs_6_), channel_id=1, source_target_pairs={{0,8},{8,0},{16,24},{24,16},{1,9},{9,1},{17,25},{25,17},{2,10},{10... | collective-permute-start | bytes 3145736 | tf_op jit(solution)/shard_map/ppermute | solution.py:322
  180.4 24.9 %collective-permute-start.20 = (bf16[256,512]{1,0:T(8,128)(2,1)S(1)}, bf16[256,512]{1,0:T(8,128)(2,1)S(1)}, u32[]{:S(2)}, u32[]{:S(2)}) collective-permute-start(bf16[256,512]{1,0:T(8,128)(2,1)S(1)} %broadcast_select_fusion.2), channel_id=1, source_target_pairs={{0,2},{1,3},{2,0},{3,1},{4,6},{5,7},{6,4},{7,5},{8,10},{9,11},{10,... | collective-permute-start | bytes 786440 | tf_op jit(solution)/shard_map/ppermute | solution.py:322
  196.0 24.1 %collective-permute-start.27 = (bf16[256,2048]{1,0:T(8,128)(2,1)}, bf16[256,2048]{1,0:T(8,128)(2,1)S(1)}, u32[]{:S(2)}, u32[]{:S(2)}) collective-permute-start(bf16[256,2048]{1,0:T(8,128)(2,1)} %collective-permute-done.25.refs_7_), channel_id=1, source_target_pairs={{0,8},{8,0},{16,24},{24,16},{1,9},{9,1},{17,25},{25,17},{2,10},{10... | collective-permute-start | bytes 3145736 | tf_op jit(solution)/shard_map/ppermute | solution.py:322
  205.2 14.8 %collective-permute-start.31 = (bf16[128,2048]{1,0:T(8,128)(2,1)S(1)}, bf16[128,2048]{1,0:T(8,128)(2,1)S(1)}, u32[]{:S(2)}, u32[]{:S(2)}) collective-permute-start(bf16[128,2048]{1,0:T(8,128)(2,1)S(1)} %get-tuple-element.66), channel_id=1, source_target_pairs={{0,1},{1,0},{2,3},{3,2},{4,5},{5,4},{6,7},{7,6},{8,9},{9,8},{10,11... | collective-permute-start | bytes 1572872 | tf_op jit(solution)/shard_map/ppermute | solution.py:322
  211.1 21.3 %collective-permute-start.24 = (bf16[128,2048]{1,0:T(8,128)(2,1)S(1)}, bf16[128,2048]{1,0:T(8,128)(2,1)S(1)}, u32[]{:S(2)}, u32[]{:S(2)}) collective-permute-start(bf16[128,2048]{1,0:T(8,128)(2,1)S(1)} %get-tuple-element.57), channel_id=1, source_target_pairs={{0,1},{1,0},{2,3},{3,2},{4,5},{5,4},{6,7},{7,6},{8,9},{9,8},{10,11... | collective-permute-start | bytes 1572872 | tf_op jit(solution)/shard_map/ppermute | solution.py:322
  225.3 17.2 %collective-permute-start.32 = (bf16[128,2048]{1,0:T(8,128)(2,1)S(1)}, bf16[128,2048]{1,0:T(8,128)(2,1)S(1)}, u32[]{:S(2)}, u32[]{:S(2)}) collective-permute-start(bf16[128,2048]{1,0:T(8,128)(2,1)S(1)} %get-tuple-element.68), channel_id=1, source_target_pairs={{0,1},{1,0},{2,3},{3,2},{4,5},{5,4},{6,7},{7,6},{8,9},{9,8},{10,11... | collective-permute-start | bytes 1572872 | tf_op jit(solution)/shard_map/ppermute | solution.py:322
  230.4 22.9 %collective-permute-start.28 = (bf16[128,2048]{1,0:T(8,128)(2,1)S(1)}, bf16[128,2048]{1,0:T(8,128)(2,1)S(1)}, u32[]{:S(2)}, u32[]{:S(2)}) collective-permute-start(bf16[128,2048]{1,0:T(8,128)(2,1)S(1)} %get-tuple-element.63), channel_id=1, source_target_pairs={{0,1},{1,0},{2,3},{3,2},{4,5},{5,4},{6,7},{7,6},{8,9},{9,8},{10,11... | collective-permute-start | bytes 1572872 | tf_op jit(solution)/shard_map/ppermute | solution.py:322
  (17 other events, 110.4 us)
Sparse Core Ops, SparseCore 0:
  13.9 56.8 all-gather.4
  73.8 57.5 all-gather.6
